TPU v7x, 32 devices: a whole 2x2x4 slice. The times are simulated.
32 devices in a mesh: dp: 8 (over y, x, core), fsdp: 4 (over z).
Axes of the slice: x: 2, y: 2, z: 4, core: 2. Of those that a mesh axis runs over, the one named last changes fastest.
Arguments:
- source: bfloat16 [32768, 512], P(('dp', 'fsdp')), may hold values from -6 to 6
- target: bfloat16 [32768, 512], P(('dp', 'fsdp')), may hold values from -6 to 6
- source_segments: int32 [64, 512], P(('dp', 'fsdp')), may hold values from 0 to 7, never falling along the last dimension, each value on 1 to 256 neighbouring positions
- target_segments: int32 [64, 512], P(('dp', 'fsdp')), may hold values from 0 to 7, never falling along the last dimension, each value on 1 to 256 neighbouring positions
- target_language: int32 [64, 8], P(('dp', 'fsdp')), may hold values from 0 to 7
- cotangent: bfloat16 [32768, 512], P(('dp', 'fsdp')), may hold values from -6 to 6
- enc_qkv: bfloat16 [512, 1536], P(('dp', 'fsdp')), may hold values from -0.25 to 0.25
- enc_out: bfloat16 [512, 512], P(('dp', 'fsdp')), may hold values from -0.5 to 0.5
- enc_up: bfloat16 [512, 2048], P(('dp', 'fsdp')), may hold values from -0.25 to 0.25
- enc_down: bfloat16 [2048, 512], P(('dp', 'fsdp')), may hold values from -0.125 to 0.125
- enc_vecs: bfloat16 [512, 8], P(('dp', 'fsdp')), may hold values from -1.2 to 1.45, as said below
- enc_bias_up: bfloat16 [2048], P(('dp', 'fsdp')), may hold values from -2 to 2
- dec_qkv: bfloat16 [512, 1536], P(('dp', 'fsdp')), may hold values from -0.25 to 0.25
- dec_out: bfloat16 [512, 512], P(('dp', 'fsdp')), may hold values from -0.5 to 0.5
- cross_q: bfloat16 [512, 512], P(('dp', 'fsdp')), may hold values from -0.25 to 0.25
- cross_kv: bfloat16 [512, 1024], P(('dp', 'fsdp')), may hold values from -0.25 to 0.25
- cross_out: bfloat16 [512, 512], P(('dp', 'fsdp')), may hold values from -0.5 to 0.5
- dec_up: bfloat16 [512, 2048], P(('dp', 'fsdp')), may hold values from -0.25 to 0.25
- dec_down: bfloat16 [2048, 512], P(('dp', 'fsdp')), may hold values from -0.125 to 0.125
- dec_vecs: bfloat16 [512, 13], P(('dp', 'fsdp')), may hold values from -1.2 to 1.45, as said below
- dec_bias_up: bfloat16 [2048], P(('dp', 'fsdp')), may hold values from -2 to 2
- lang_table: bfloat16 [512, 8], P(('dp', 'fsdp')), may hold values from -4 to 4
Outputs:
- dec_output: bfloat16 [32768, 512], P(('dp', 'fsdp'))
- source_grad: bfloat16 [32768, 512], P(('dp', 'fsdp'))
- target_grad: bfloat16 [32768, 512], P(('dp', 'fsdp'))
- enc_qkv_grad: float32 [512, 1536], P(('dp', 'fsdp'))
- enc_out_grad: float32 [512, 512], P(('dp', 'fsdp'))
- enc_up_grad: float32 [512, 2048], P(('dp', 'fsdp'))
- enc_down_grad: float32 [2048, 512], P(('dp', 'fsdp'))
- enc_vecs_grad: float32 [512, 8], P(('dp', 'fsdp'))
- enc_bias_up_grad: float32 [2048], P(('dp', 'fsdp'))
- dec_qkv_grad: float32 [512, 1536], P(('dp', 'fsdp'))
- dec_out_grad: float32 [512, 512], P(('dp', 'fsdp'))
- cross_q_grad: float32 [512, 512], P(('dp', 'fsdp'))
- cross_kv_grad: float32 [512, 1024], P(('dp', 'fsdp'))
- cross_out_grad: float32 [512, 512], P(('dp', 'fsdp'))
- dec_up_grad: float32 [512, 2048], P(('dp', 'fsdp'))
- dec_down_grad: float32 [2048, 512], P(('dp', 'fsdp'))
- dec_vecs_grad: float32 [512, 13], P(('dp', 'fsdp'))
- dec_bias_up_grad: float32 [2048], P(('dp', 'fsdp'))
- lang_table_grad: float32 [512, 8], P(('dp', 'fsdp'))
Inputs may be any that keep to these rules, and one draw needn't show every extreme that they name: `source_segments`: within each row the numbers never fall; each of the 8 sentences holds 1 to 256 positions, and one holds exactly 256. `target_segments`: within each row the numbers never fall; each of the 8 sentences holds 1 to 256 positions, and one holds exactly 256. `enc_vecs`: columns 3 and 6 are gains, the others biases. `dec_vecs`: columns 3, 8 and 11 are gains, the others biases.
All inputs are finite; a program needn't handle non-finite values.
Results may differ from a plain program's by a relative error of at most 0.023.
Values may be sent and summed in bfloat16 or wider, within the bound.
No kernel may reach another device: no remote copies, remote signals or barrier semaphores. Data moves between devices by JAX's collectives and lax.ppermute only.
A program may use at most 256 MiB of HBM per device.

v0:
```python
import functools

import jax
import jax.numpy as jnp
from jax import lax
from jax.experimental import pallas as pl
from jax.experimental.pallas import tpu as pltpu
from jax.sharding import PartitionSpec as P

AXES = ("dp", "fsdp")
LANGS = 8
ROW = 512
CHUNK = 512
scale_dot = 0.125
norm_eps = 1e-05

ENC = 8
DEC = 16
ENC_UP = 29
DEC_UP = 33
SMALL = ((0, 8), (8, 8), (16, 13), (29, 4), (33, 4))
BF = jnp.bfloat16
F32 = jnp.float32


class Grid:
    def __init__(self, mesh):
        self.nd = mesh.shape["dp"]
        self.nf = mesh.shape["fsdp"]
        self.n = self.nd * self.nf
        self.nh = self.nd // 2
        self.hz = self.nh * self.nf
        self.unit = ROW // self.n
        self.tiled = self.unit % 16 == 0
        self.cut = (self.n, self.unit) if self.tiled else (32, 16)

    def me(self):
        return lax.axis_index("dp") * self.nf + lax.axis_index("fsdp")

    def swap_dp(self, value, flip):
        return lax.ppermute(value, "dp", [(i, i ^ flip) for i in range(self.nd)])

    def swap_fsdp(self, value, flip):
        return lax.ppermute(value, "fsdp", [(i, i ^ flip) for i in range(self.nf)])

    def relative(self, part, at):
        return (at // self.nf * 2 + part) * self.nf + at % self.nf

    def spot(self, me, part, at, across):
        if not across:
            return jnp.bitwise_xor(me, self.relative(part, at))
        flip = (at // self.nf * 2 + part) * self.nf
        return jnp.bitwise_xor(me - lax.rem(me, self.nf), flip) + at % self.nf


def after(value, token):
    if token is None:
        return value
    return lax.optimization_barrier((value, token))[0]


def z_copies(grid, shard):
    return lax.all_to_all(
        jnp.broadcast_to(shard[None], (grid.nf,) + shard.shape), "fsdp", 0, 0, tiled=False
    )


def z_gather(grid, shard):
    return [shard] + [grid.swap_fsdp(shard, m) for m in range(1, grid.nf)]


def z_gather_halves(grid, shard):
    order = [0]
    flips = [1 << b for b in range(grid.nf.bit_length() - 1)]
    held = shard[None]
    for flip in reversed(flips):
        held = jnp.concatenate([held, grid.swap_fsdp(held, flip)])
        order = order + [o | flip for o in order]
    return jnp.stack([held[order.index(z)] for z in range(grid.nf)])


def xy_gather(grid, held):
    return [held] + [grid.swap_dp(held, h << 1) for h in range(1, grid.nh)]


def xy_gather_early(grid, held):
    return [held] + [grid.swap_dp(held, h << 1) for h in range(1, grid.nh - 1)]


def xy_gather_rest(grid, held):
    return [grid.swap_dp(held, grid.nh - 1 << 1)]


def core_sum(grid, keep, got):
    shape = (grid.nh, grid.nf) + keep.shape[1:]
    keep, got = keep.reshape(shape), got.reshape(shape)
    kind = keep.dtype
    sends = [(keep[h].astype(F32) + got[h].astype(F32)).astype(kind) for h in range(1, grid.nh)]
    return [keep[0], got[0]], sends


def xy_scatter(grid, sends):
    return [grid.swap_dp(s, h << 1) for h, s in zip(range(1, grid.nh), sends)]


def xy_sum(grid, parts, z):
    out = parts[0][z].astype(F32)
    for part in parts[1:]:
        out = out + part[z].astype(F32)
    return out


class Piece:
    def __init__(self, grid, forms, plain=False, across=False):
        self.grid, self.forms, self.plain, self.across = grid, forms, plain, across
        self.starts = [sum(b for b, _ in forms[:k]) for k in range(len(forms))]
        self.blocks = sum(b for b, _ in forms)
        self.refs = 1 if plain or not grid.tiled else 2

    def cut(self, k):
        blocks, wide = self.forms[k]
        a, b = self.grid.cut
        return (a, blocks, b, 512) if wide is False else (blocks, a, b, 512)

    def arrive(self, *held):
        grid = self.grid
        if grid.tiled:
            shape = (-1, self.blocks, grid.unit, 512)
            self.arrays = [tuple(near_not(h.reshape(shape)) for h in held)] * len(self.forms)
            return
        whole = jnp.concatenate(held)
        if not self.plain:
            spots = [
                grid.spot(grid.me(), part, at, self.across)
                for part in range(2)
                for at in range(grid.hz)
            ]
            index = jnp.zeros((grid.n,), jnp.int32).at[jnp.stack(spots)].set(
                jnp.arange(grid.n, dtype=jnp.int32)
            )
            whole = jnp.take(whole, index, axis=0)
        self.arrays = []
        for k, (blocks, wide) in enumerate(self.forms):
            row = self.starts[k] * grid.unit
            part = whole[:, row : row + blocks * grid.unit]
            if wide is not False:
                part = part.reshape(grid.n, blocks, grid.unit, 512).transpose(1, 0, 2, 3)
            self.arrays.append((part.reshape(self.cut(k)),))

    def pairs(self, k, me, refs, held):
        grid = self.grid
        blocks, wide = self.forms[k]
        start = self.starts[k]
        if not grid.tiled:
            yield refs[0 if len(refs) == 1 else k], held
        elif self.plain and wide is not False:
            for j in range(blocks):
                yield refs[0].at[:, start + j], held.at[j]
        elif self.plain:
            yield refs[0].at[:, pl.ds(start, blocks)], held
        else:
            for part, ref in enumerate(refs):
                for at in range(grid.hz):
                    i = grid.spot(me, part, at, self.across)
                    yield ref.at[at, pl.ds(start, blocks)], held.at[i] if wide is False else held.at[:, i]

    def fetch(self, k, me, refs, dst, sem):
        for there, here in self.pairs(k, me, refs, dst):
            pltpu.make_async_copy(there, here, sem).start()

    def store(self, k, me, src, refs, sem):
        for there, here in self.pairs(k, me, refs, src):
            pltpu.make_async_copy(here, there, sem).start()

    def out_shapes(self):
        grid = self.grid
        if not grid.tiled:
            return [jax.ShapeDtypeStruct(self.cut(k), BF) for k in range(len(self.forms))]
        if self.plain:
            return [jax.ShapeDtypeStruct((grid.n, self.blocks, grid.unit, 512), BF)]
        return [jax.ShapeDtypeStruct((grid.hz, self.blocks, grid.unit, 512), BF)] * 2

    def ready(self, outs):
        grid = self.grid
        rows = self.blocks * grid.unit
        if grid.tiled:
            return [out.reshape(-1, rows, 512) for out in outs]
        parts = []
        for k, (blocks, wide) in enumerate(self.forms):
            part = outs[k]
            if wide is not False:
                part = part.reshape(blocks, grid.n, grid.unit, 512).transpose(1, 0, 2, 3)
            parts.append(part.reshape(grid.n, blocks * grid.unit, 512))
        whole = jnp.concatenate(parts, axis=1)
        return [whole] if self.plain else spread_blocks(grid, whole)


def scatter_plain(grid, whole):
    rows = whole.shape[1]
    part = lax.psum_scatter(
        whole.reshape(grid.nd, grid.nf * rows, 512), "dp", scatter_dimension=0, tiled=False
    )
    return lax.psum_scatter(
        part.reshape(grid.nf, rows, 512), "fsdp", scatter_dimension=0, tiled=False
    )


def spread_blocks(grid, whole):
    sides = []
    for part in range(2):
        table = [grid.relative(part, at) for at in range(grid.hz)]
        sides.append(jnp.take(whole, jnp.array(table, jnp.int32) ^ grid.me(), axis=0))
    return sides


def finish(ref, sem):
    pltpu.make_async_copy(ref, ref, sem).wait()


def to_rows(shard):
    unit = shard.shape[0]
    blocks = shard.shape[1] // 512
    return shard.reshape(unit, blocks, 512).transpose(1, 0, 2).reshape(blocks * unit, 512)


def fours(rows, start, width):
    k = lax.broadcasted_iota(jnp.int32, (4 * rows, width), 0)
    return lax.broadcasted_iota(jnp.int32, (4 * rows, width), 1) == start + lax.rem(k, 4)


def own_row(rows):
    k = lax.broadcasted_iota(jnp.int32, (rows, 4 * rows), 1)
    return lax.broadcasted_iota(jnp.int32, (rows, 4 * rows), 0) == k // 4


def flatten_fours(value, start):
    rows = value.shape[0]
    wide = lax.dot_general(
        value,
        fours(rows, start, 128).astype(F32),
        (((1,), (1,)), ((), ())),
        precision=lax.Precision.HIGHEST,
        preferred_element_type=F32,
    )
    return jnp.sum(jnp.where(own_row(rows), wide, 0.0), axis=0, keepdims=True)


def place_small(parts, rows):
    total = None
    for (start, width), part in zip(SMALL, parts):
        value = part[...]
        if width == 4:
            value = jnp.where(own_row(rows), value.astype(F32), 0.0).astype(BF)
            spots = fours(rows, start, 512)
        else:
            r = lax.broadcasted_iota(jnp.int32, (width, 512), 0)
            spots = lax.broadcasted_iota(jnp.int32, (width, 512), 1) == start + r
        value = jnp.dot(value, jnp.where(spots, 1.0, 0.0).astype(BF), preferred_element_type=F32)
        total = value if total is None else total + value
    return total.astype(BF)


def pack_kernel(counts, unit, *refs):
    refs = list(refs)
    small = [refs.pop(0) for _ in SMALL]
    groups = [[refs.pop(0) for _ in range(count)] for count in counts]
    refs[0][4 * unit : 5 * unit] = place_small(small, unit)
    for group, out in zip(groups, refs):
        at = 0
        for ref in group:
            rows = ref.shape[0]
            for j in range(ref.shape[1] // 512):
                if out is refs[0] and at == 4 * unit:
                    at += unit
                out[at : at + rows] = ref[:, 512 * j : 512 * (j + 1)]
                at += rows


def pack(grid, small, *groups):
    if not grid.tiled:
        flat = [p.reshape(grid.unit, 4) if w == 4 else p for (_, w), p in zip(SMALL, small)]
        flat = jnp.concatenate(flat, axis=1)
        flat = jnp.pad(flat, ((0, 0), (0, 512 - flat.shape[1])))
        first, *rest = groups
        groups = [list(first[:2]) + [flat] + list(first[2:])] + rest
        return [
            jnp.concatenate([to_rows(a) if a.shape[0] == grid.unit else a for a in arrays])
            for arrays in groups
        ]
    rows = [sum(a.size for a in arrays) // 512 for arrays in groups]
    rows[0] += grid.unit
    flat = [p.reshape(1, -1) if w == 4 else p for (_, w), p in zip(SMALL, small)]
    return pl.pallas_call(
        functools.partial(pack_kernel, [len(arrays) for arrays in groups], grid.unit),
        out_shape=[like(r, 512, BF) for r in rows],
        compiler_params=params(56),
        name="pack",
    )(*flat, *[a for arrays in groups for a in arrays])


def shards_kernel(pieces, counts, *refs):
    refs = list(refs)
    own = [[refs.pop(0) for _ in range(count)] for count in counts[:-1]]
    lasts = [refs.pop(0) for _ in range(counts[-1])]
    at = 0
    for piece, parts in zip(pieces, own):
        rows = piece.blocks * piece.grid.unit
        total = None
        for part in parts:
            total = part[0].astype(F32) if total is None else total + part[0].astype(F32)
        for last in lasts:
            total = total + last[at : at + rows].astype(F32)
        at += rows
        row, unit = 0, piece.grid.unit
        for blocks, wide in piece.forms:
            if wide is None:
                value = total[row : row + unit]
                for start, width in SMALL:
                    out = refs.pop(0)
                    if width == 4:
                        out[...] = flatten_fours(value[:, :128], start)
                    else:
                        out[...] = value[:, start : start + width]
                row += unit
                continue
            out = refs.pop(0)
            for j in range(blocks):
                value = total[row : row + unit]
                if wide:
                    out[:, 512 * j : 512 * (j + 1)] = value
                else:
                    out[unit * j : unit * (j + 1)] = value
                row += unit


def shards(grid, pieces, own, lasts):
    if not grid.tiled:
        total = jnp.concatenate(
            [functools.reduce(lambda a, b: a + b, [p[0].astype(F32) for p in parts]) for parts in own]
        )
        for last in lasts:
            total = total + last.astype(F32)
        outs, row = [], 0
        for piece in pieces:
            for blocks, wide in piece.forms:
                part = total[row : row + blocks * grid.unit]
                if wide is None:
                    outs += [part[:, start : start + width] for start, width in SMALL]
                else:
                    outs.append(from_rows(part, blocks) if wide else part)
                row += blocks * grid.unit
        return outs
    first = lambda a: pl.BlockSpec((1,) + a.shape[1:], lambda i: (0, 0, 0))
    args = [a for parts in own for a in parts] + lasts
    specs = [first(a) for parts in own for a in parts] + [whole_spec(a) for a in lasts]
    shapes = []
    for piece in pieces:
        for blocks, wide in piece.forms:
            if wide is None:
                shapes += [
                    like(1, grid.unit * 4, F32) if width == 4 else like(grid.unit, width, F32)
                    for _, width in SMALL
                ]
            elif wide:
                shapes.append(like(grid.unit, 512 * blocks, F32))
            else:
                shapes.append(like(grid.unit * blocks, 512, F32))
    return pl.pallas_call(
        functools.partial(shards_kernel, pieces, [len(p) for p in own] + [len(lasts)]),
        grid=(1,),
        in_specs=specs,
        out_specs=[whole_spec(s) for s in shapes],
        out_shape=shapes,
        compiler_params=params(56),
        name="shards",
    )(*args)


def from_rows(rows, blocks):
    unit = rows.shape[0] // blocks
    return rows.reshape(blocks, unit, 512).transpose(1, 0, 2).reshape(unit, blocks * 512)


HALF = 64
BIG = float(2**30)


def dot(a, b):
    return jnp.dot(a, b, preferred_element_type=jnp.float32)


def dot_t(a, b):
    return lax.dot_general(a, b, (((1,), (1,)), ((), ())), preferred_element_type=jnp.float32)


def t_dot(a, b):
    return lax.dot_general(a, b, (((0,), (0,)), ((), ())), preferred_element_type=jnp.float32)


def lanes(rows=1, width=128):
    return lax.broadcasted_iota(jnp.int32, (rows, width), 1)


def head_lanes(h):
    return jnp.where(lanes() // HALF == h, 1.0, 0.0).astype(jnp.bfloat16)


def one_lanes(h):
    at = lanes() - HALF * h
    return jnp.where((at >= 8) & (at < 11), 1.0, 0.0).astype(jnp.bfloat16)


def minus_parts(value):
    at = lanes() % HALF
    value = -value
    high = value.astype(jnp.bfloat16).astype(jnp.float32)
    rest = value - high
    mid = rest.astype(jnp.bfloat16).astype(jnp.float32)
    low = rest - mid
    out = jnp.where(at == 8, high, jnp.where(at == 9, mid, jnp.where(at == 10, low, 0.0)))
    return out.astype(jnp.bfloat16)


def pair(value, p):
    return value[:, 128 * p : 128 * (p + 1)]


def norm(summed):
    centred = summed - jnp.mean(summed, axis=-1, keepdims=True)
    inverse = lax.rsqrt(jnp.mean(centred * centred, axis=-1, keepdims=True) + norm_eps)
    return centred * inverse, inverse


def heads_forward(q, k, v, hot, bar):
    outs, logs = [], []
    for p in range(q.shape[1] // 128):
        qa = jnp.concatenate([pair(q, p) * jnp.bfloat16(scale_dot), hot], axis=1)
        total, tops = None, []
        for h in (0, 1):
            mask = head_lanes(h)
            ka = jnp.concatenate([pair(k, p) * mask, bar], axis=1)
            scores = dot_t(qa, ka)
            top = jnp.max(scores, axis=-1, keepdims=True)
            power = jnp.exp(scores - top).astype(jnp.bfloat16)
            va = jnp.concatenate(
                [pair(v, p) * mask, jnp.broadcast_to(mask, (v.shape[0], 128))], axis=1
            )
            part = dot(power, va)
            total = part if total is None else total + part
            tops.append(top)
        sums = total[:, 128:]
        outs.append(total[:, :128] / sums)
        logs.append(jnp.where(lanes() < HALF, tops[0], tops[1]) + jnp.log(sums))
    return jnp.concatenate(outs, axis=1), jnp.concatenate(logs, axis=1)


def heads_backward(go, q, k, v, o, lse, hot, bar):
    gqs, gks, gvs = [], [], []
    at = lax.broadcasted_iota(jnp.int32, (128, 128), 0) // HALF
    to = lax.broadcasted_iota(jnp.int32, (128, 128), 1) // HALF
    same = jnp.where(at == to, 1.0, 0.0).astype(jnp.bfloat16)
    same = jnp.concatenate([same, same], axis=0)
    for p in range(q.shape[1] // 128):
        qs = pair(q, p) * jnp.bfloat16(scale_dot)
        gp = pair(go, p)
        prod = gp.astype(jnp.float32) * pair(o, p)
        high = prod.astype(jnp.bfloat16)
        low = (prod - high.astype(jnp.float32)).astype(jnp.bfloat16)
        delta = dot(jnp.concatenate([high, low], axis=1), same)
        qa = jnp.concatenate([qs, hot + minus_parts(pair(lse, p))], axis=1)
        ga = jnp.concatenate([gp, minus_parts(delta)], axis=1)
        gq = gk = gv = None
        for h in (0, 1):
            mask, one = head_lanes(h), one_lanes(h)
            km = pair(k, p) * mask
            ka = jnp.concatenate([km, bar + one], axis=1)
            va = jnp.concatenate(
                [pair(v, p) * mask, jnp.broadcast_to(one, (v.shape[0], 128))], axis=1
            )
            probs = jnp.exp(dot_t(ka, qa))
            gs = (probs * dot_t(va, ga)).astype(jnp.bfloat16)
            gv_h = dot(probs.astype(jnp.bfloat16), gp * mask)
            gk_h = dot(gs, qs * mask)
            gq_h = t_dot(gs, km)
            gv = gv_h if gv is None else gv + gv_h
            gk = gk_h if gk is None else gk + gk_h
            gq = gq_h if gq is None else gq + gq_h
        gqs.append((gq * scale_dot).astype(jnp.bfloat16))
        gks.append(gk.astype(jnp.bfloat16))
        gvs.append(gv.astype(jnp.bfloat16))
    return tuple(jnp.concatenate(x, axis=1) for x in (gqs, gks, gvs))


def norm_back(grad, normed, inverse, gain):
    scaled = grad * gain
    back = inverse * (
        scaled
        - jnp.mean(scaled, axis=-1, keepdims=True)
        - normed * jnp.mean(scaled * normed, axis=-1, keepdims=True)
    )
    return back, jnp.sum(grad * normed, axis=0), jnp.sum(grad, axis=0)


def square(ref, k):
    return ref[k].reshape(512, 512)


def vec(vectors, k):
    return vectors[k : k + 1, :]


ANY = pl.BlockSpec(memory_space=pl.ANY)
SMEM = pl.BlockSpec(memory_space=pltpu.SMEM)


def whole_spec(array):
    return pl.BlockSpec(array.shape, lambda i: (0,) * array.ndim)


def row_spec(array):
    return pl.BlockSpec((ROW,) + array.shape[1:], lambda i: (i,) + (0,) * (array.ndim - 1))


def near_not(array):
    return pltpu.with_memory_space_constraint(array, pltpu.HBM)


def far(shape):
    return pltpu.HBM(shape.shape, shape.dtype)


def like(rows, width, kind):
    return jax.ShapeDtypeStruct((rows, width), kind)


def params(mebibytes):
    return pltpu.CompilerParams(vmem_limit_bytes=mebibytes * 1024 * 1024)


def cost(tokens, macs):
    return pl.CostEstimate(
        flops=2 * tokens * macs, bytes_accessed=16 * tokens * 512, transcendentals=0
    )


def attend_forward_kernel(mode, base, piece, small, *refs):
    refs = list(refs)
    me_ref = refs.pop(0)
    count = piece.refs
    take = lambda k: [refs.pop(0) for _ in range(k)]
    proj_refs = [take(count) for _ in range(3 if mode == "cross" else 2)]
    small_refs = take(count) if small is not None else None
    vectors_ref = None if small is not None else refs.pop(0)
    if mode == "cross":
        normed_ref, memory_ref = take(2)
    else:
        x_ref = refs.pop(0)
        if mode == "dec":
            lang_ref = refs.pop(0)
    hot_ref, bar_ref = take(2)
    q_out, k_out, v_out, o_out, lse_out, n_out, inv_out = take(7)
    if mode != "enc":
        low_out = refs.pop(0)
    if small is not None:
        vectors_out, small_out = take(2)
    weights = take(3 if mode == "cross" else 2)
    small_scr = refs.pop(0) if small is not None else None
    sems = refs.pop(0)
    out_w = weights[-1]

    @pl.when(pl.program_id(0) == 0)
    def _():
        me = me_ref[0]
        for k, (source, dst) in enumerate(zip(proj_refs, weights)):
            piece.fetch(k, me, source, dst, sems.at[k])
        if small is not None:
            piece.fetch(small, me, small_refs, small_scr, sems.at[3])
            finish(small_scr, sems.at[3])
            block = small_scr[0].reshape(512, 512)[:, :128]
            small_out[...] = block
            vectors_out[...] = block.astype(F32).T
        for k, dst in enumerate(weights):
            finish(dst, sems.at[k])

    vectors = (vectors_out if small is not None else vectors_ref)[...]
    if mode == "enc":
        low = x_ref[...]
        residual = low.astype(F32)
        memory = low
    elif mode == "dec":
        residual = x_ref[...].astype(F32) + dot(lang_ref[...], vectors.astype(BF))
        low = memory = residual.astype(BF)
    else:
        residual = normed_ref[...] * vec(vectors, DEC + 3) + vec(vectors, DEC + 4)
        low = residual.astype(BF)
        memory = memory_ref[...]
    if mode != "enc":
        low_out[...] = low
    if mode == "cross":
        wq, wk, wv = square(weights[0], 0), square(weights[1], 0), square(weights[1], 1)
    else:
        wq, wk, wv = (square(weights[0], j) for j in range(3))
    q = (dot(low, wq) + vec(vectors, base)).astype(BF)
    k = dot(memory, wk).astype(BF)
    v = (dot(memory, wv) + vec(vectors, base + 1)).astype(BF)
    q_out[...], k_out[...], v_out[...] = q, k, v
    o, lse = heads_forward(q, k, v, hot_ref[...], bar_ref[...])
    o_out[...], lse_out[...] = o, lse
    branch = dot(o.astype(BF), square(out_w, 0)) + vec(vectors, base + 2)
    n_out[...], inv_out[...] = norm(residual + branch)


def attend_forward(mode, base, me, piece, small, inputs, hot, bar, vectors):
    grid = piece.grid
    tokens = hot.shape[0]
    names = range(3 if mode == "cross" else 2)
    weights = [a for k in names for a in piece.arrays[k]]
    args = [me] + weights
    specs = [SMEM] + [ANY] * len(weights)
    if small is not None:
        args += list(piece.arrays[small])
        specs += [ANY] * len(piece.arrays[small])
    else:
        args.append(vectors)
        specs.append(whole_spec(vectors))
    rows = [near_not(inputs[0])] + list(inputs[1:]) + [hot, bar]
    args += rows
    specs += [row_spec(a) for a in rows]
    outs = [like(tokens, 512, BF)] * 3 + [like(tokens, 512, F32)] * 3 + [like(tokens, 1, F32)]
    if mode != "enc":
        outs.append(like(tokens, 512, BF))
    out_specs = [row_spec(o) for o in outs]
    outs = [o if i == 5 and mode == "cross" else far(o) for i, o in enumerate(outs)]
    scratch = [pltpu.VMEM(piece.cut(k), BF) for k in names]
    if small is not None:
        extra = [like(128, 512, F32), like(512, 128, BF)]
        outs += extra
        out_specs += [whole_spec(e) for e in extra]
        scratch.append(pltpu.VMEM(piece.cut(small), BF))
    scratch.append(pltpu.SemaphoreType.DMA((4,)))
    return pl.pallas_call(
        functools.partial(attend_forward_kernel, mode, base, piece, small),
        grid=(tokens // ROW,),
        in_specs=specs,
        out_specs=out_specs,
        out_shape=outs,
        scratch_shapes=scratch,
        compiler_params=params(24),
        cost_estimate=cost(tokens, 4 * 512 * 512 + 2 * 8 * 512 * 256),
        name="attend_forward_" + mode,
    )(*args)


def feed_forward_kernel(base, first, piece, own, *refs):
    refs = list(refs)
    me_ref = refs.pop(0)
    count = piece.refs
    take = lambda k: [refs.pop(0) for _ in range(k)]
    up_refs, down_refs = take(count), take(count)
    vectors_ref, bias_ref, n_ref = take(3)
    act_out, slope_out, n_out, inv_out, low_out = take(5)
    up, down, sems = take(3)

    @pl.when(pl.program_id(0) == 0)
    def _():
        me = me_ref[0]
        piece.fetch(own, me, up_refs, up, sems.at[0])
        piece.fetch(own + 1, me, down_refs, down, sems.at[1])
        finish(up, sems.at[0])
        finish(down, sems.at[1])

    vectors = vectors_ref[...]
    x = n_ref[...] * vec(vectors, first) + vec(vectors, first + 1)
    low = x.astype(BF)
    branch = None
    for j in range(4):
        h = dot(low, square(up, j)) + bias_ref[j : j + 1, :]
        act, slope = gate(h)
        act = act.astype(BF)
        act_out[j], slope_out[j] = act, slope.astype(BF)
        part = dot(act, tall(down, j))
        branch = part if branch is None else branch + part
    n, inv = norm(x + branch + vec(vectors, base))
    n_out[...], inv_out[...] = n, inv
    low_out[...] = (n * vec(vectors, base + 1) + vec(vectors, base + 2)).astype(BF)


def gate(h):
    c = 0.7978845608028654
    square_h = h * h
    t = jnp.tanh(h * (c + (c * 0.044715) * square_h))
    half = 0.5 + 0.5 * t
    slope = half + (0.5 * h) * (1.0 - t * t) * (c + (3.0 * c * 0.044715) * square_h)
    return h * half, slope


def tall(ref, j):
    size = ref.shape[0] // 4
    return ref[size * j : size * (j + 1)].reshape(512, 512)


def feed_forward(base, first, me, piece, own, vectors, bias, n):
    tokens = n.shape[0]
    weights = list(piece.arrays[own]) + list(piece.arrays[own + 1])
    chunk = jax.ShapeDtypeStruct((4, tokens, 512), BF)
    chunk_spec = pl.BlockSpec((4, ROW, 512), lambda i: (0, i, 0))
    outs = [chunk, chunk, like(tokens, 512, F32), like(tokens, 1, F32), like(tokens, 512, BF)]
    out_specs = [chunk_spec, chunk_spec] + [row_spec(o) for o in outs[2:]]
    outs = [far(o) for o in outs[:4]] + outs[4:]
    return pl.pallas_call(
        functools.partial(feed_forward_kernel, base, first, piece, own),
        grid=(tokens // ROW,),
        in_specs=[SMEM]
        + [ANY] * len(weights)
        + [whole_spec(vectors), whole_spec(bias), row_spec(n)],
        out_specs=out_specs,
        out_shape=outs,
        scratch_shapes=[
            pltpu.VMEM(piece.cut(own), BF),
            pltpu.VMEM(piece.cut(own + 1), BF),
            pltpu.SemaphoreType.DMA((2,)),
        ],
        compiler_params=params(26),
        cost_estimate=cost(tokens, 8 * 512 * 512),
        name="feed_forward",
    )(me, *weights, vectors, bias, near_not(n))


def feed_backward_kernel(base, first, piece, own, grads, at, *refs):
    refs = list(refs)
    me_ref = refs.pop(0)
    count = piece.refs
    take = lambda k: [refs.pop(0) for _ in range(k)]
    up_refs, down_refs = take(count), take(count)
    vectors_ref, grad_ref, n2_ref, inv2_ref, n1_ref, act_ref, slope_ref = take(7)
    grad_outs = take(len(grads.out_shapes()))
    dx_out, sums_out, bias_out = take(3)
    up, down, d_up, d_down, low_t, branch, sems = take(7)
    j = pl.program_id(0)
    vectors = vectors_ref[...]

    @pl.when(j == 0)
    def _():
        me = me_ref[0]
        piece.fetch(own, me, up_refs, up, sems.at[0])
        piece.fetch(own + 1, me, down_refs, down, sems.at[1])
        sums_out[...] = jnp.zeros_like(sums_out)
        for t in range(grad_ref.shape[0] // ROW):
            part = pl.ds(ROW * t, ROW)
            back, gain, shift = norm_back(
                grad_ref[part].astype(F32), n2_ref[part], inv2_ref[part], vec(vectors, base + 1)
            )
            dx_out[part] = back
            low = back.astype(BF)
            branch[part] = low
            sums_out[0:1] += jnp.sum(low.astype(F32), axis=0, keepdims=True)
            sums_out[1:2] += gain[None]
            sums_out[2:3] += shift[None]
            x = n1_ref[part] * vec(vectors, first) + vec(vectors, first + 1)
            low_t[:, part] = x.astype(BF).T
        finish(up, sems.at[0])
        finish(down, sems.at[1])

    size = down.shape[0] // 4
    down_j = down[pl.ds(size * j, size)].reshape(512, 512)
    up_j = up[j].reshape(512, 512)
    low = branch[...]
    hidden = (dot_t(low, down_j) * slope_ref[0].astype(F32)).astype(BF)
    bias_out[0] = jnp.broadcast_to(
        jnp.sum(hidden.astype(F32), axis=0, keepdims=True), bias_out.shape[1:]
    )
    dx_out[...] += dot_t(hidden, up_j)
    d_up[j] = dot(low_t[...], hidden).astype(BF).reshape(d_up.shape[1:])
    d_down[pl.ds(size * j, size)] = (
        t_dot(act_ref[0], low).astype(BF).reshape((size,) + d_down.shape[1:])
    )

    @pl.when(j == pl.num_programs(0) - 1)
    def _():
        me = me_ref[0]
        grads.store(at, me, d_up, grad_outs, sems.at[0])
        grads.store(at + 1, me, d_down, grad_outs, sems.at[1])
        finish(d_up, sems.at[0])
        finish(d_down, sems.at[1])


def feed_backward(base, first, me, piece, own, grads, at, vectors, grad, n2, inv2, n1, act, slope):
    tokens = n1.shape[0]
    weights = list(piece.arrays[own]) + list(piece.arrays[own + 1])
    act, slope, n2, inv2, n1 = (near_not(a) for a in (act, slope, n2, inv2, n1))
    held = [vectors, grad, n2, inv2, n1]
    chunk_spec = pl.BlockSpec((1, tokens, 512), lambda i: (i, 0, 0))
    outs = [like(tokens, 512, F32), like(8, 512, F32), jax.ShapeDtypeStruct((4, 8, 512), F32)]
    got = pl.pallas_call(
        functools.partial(feed_backward_kernel, base, first, piece, own, grads, at),
        grid=(4,),
        in_specs=[SMEM]
        + [ANY] * len(weights)
        + [whole_spec(a) for a in held]
        + [chunk_spec, chunk_spec],
        out_specs=[ANY] * len(grads.out_shapes())
        + [whole_spec(outs[0]), whole_spec(outs[1]), pl.BlockSpec((1, 8, 512), lambda i: (i, 0, 0))],
        out_shape=[far(s) for s in grads.out_shapes()] + [far(outs[0])] + outs[1:],
        scratch_shapes=[
            pltpu.VMEM(piece.cut(own), BF),
            pltpu.VMEM(piece.cut(own + 1), BF),
            pltpu.VMEM(grads.cut(at), BF),
            pltpu.VMEM(grads.cut(at + 1), BF),
            pltpu.VMEM((512, tokens), BF),
            pltpu.VMEM((tokens, 512), BF),
            pltpu.SemaphoreType.DMA((2,)),
        ],
        compiler_params=params(32),
        cost_estimate=cost(tokens, 16 * 512 * 512),
        name="feed_backward",
    )(me, *weights, *held, act, slope)
    m = len(grads.out_shapes())
    return got[:m], got[m], got[m + 1], got[m + 2][:, 0, :]


def feed_both_kernel(base, first, piece, own, grads, at, tiles, *refs):
    refs = list(refs)
    me_ref = refs.pop(0)
    take = lambda k: [refs.pop(0) for _ in range(k)]
    up_refs, down_refs = take(piece.refs), take(piece.refs)
    vectors_ref, bias_ref, n1_ref, grad_ref = take(4)
    grad_outs = take(len(grads.out_shapes()))
    low_out, dx_out, sums_out, bias_out = take(4)
    up, down, d_up, d_down, acts, slopes, low_t, branches, sems = take(9)
    step = pl.program_id(0)
    vectors = vectors_ref[...]

    @pl.when(step == 0)
    def _():
        me = me_ref[0]
        piece.fetch(own, me, up_refs, up, sems.at[0])
        piece.fetch(own + 1, me, down_refs, down, sems.at[1])
        sums_out[...] = jnp.zeros_like(sums_out)
        finish(up, sems.at[0])
        finish(down, sems.at[1])

    @pl.when(step < tiles)
    def _():
        x = n1_ref[...] * vec(vectors, first) + vec(vectors, first + 1)
        low = x.astype(BF)
        rows = pl.ds(pl.multiple_of(step * ROW, ROW), ROW)
        branch = None
        for j in range(4):
            h = dot(low, square(up, j)) + bias_ref[j : j + 1, :]
            act, slope = gate(h)
            act = act.astype(BF)
            acts[j, rows], slopes[j, rows] = act, slope.astype(BF)
            part = dot(act, tall(down, j))
            branch = part if branch is None else branch + part
        n, inv = norm(x + branch + vec(vectors, base))
        gain = vec(vectors, base + 1)
        low_out[...] = (n * gain + vec(vectors, base + 2)).astype(BF)
        back, d_gain, d_shift = norm_back(grad_ref[...].astype(F32), n, inv, gain)
        dx_out[rows] = back
        back = back.astype(BF)
        branches[rows] = back
        sums_out[0:1] += jnp.sum(back.astype(F32), axis=0, keepdims=True)
        sums_out[1:2] += d_gain[None]
        sums_out[2:3] += d_shift[None]
        low_t[:, rows] = low.T

    @pl.when(step >= tiles)
    def _():
        j = step - tiles
        size = down.shape[0] // 4
        low = branches[...]
        hidden = dot_t(low, down[pl.ds(size * j, size)].reshape(512, 512))
        hidden = (hidden * slopes[j].astype(F32)).astype(BF)
        bias_out[0] = jnp.broadcast_to(
            jnp.sum(hidden.astype(F32), axis=0, keepdims=True), bias_out.shape[1:]
        )
        dx_out[...] += dot_t(hidden, up[j].reshape(512, 512))
        d_up[j] = dot(low_t[...], hidden).astype(BF).reshape(d_up.shape[1:])
        d_down[pl.ds(size * j, size)] = (
            t_dot(acts[j], low).astype(BF).reshape((size,) + d_down.shape[1:])
        )

    @pl.when(step == pl.num_programs(0) - 1)
    def _():
        me = me_ref[0]
        grads.store(at, me, d_up, grad_outs, sems.at[0])
        grads.store(at + 1, me, d_down, grad_outs, sems.at[1])
        finish(d_up, sems.at[0])
        finish(d_down, sems.at[1])


def feed_both(base, first, me, piece, own, grads, at, vectors, bias, n1, grad):
    tokens = n1.shape[0]
    tiles = tokens // ROW
    weights = list(piece.arrays[own]) + list(piece.arrays[own + 1])
    tile_spec = pl.BlockSpec((ROW, 512), lambda i: (jnp.minimum(i, tiles - 1), 0))
    outs = [
        like(tokens, 512, BF),
        like(tokens, 512, F32),
        like(8, 512, F32),
        jax.ShapeDtypeStruct((4, 8, 512), F32),
    ]
    got = pl.pallas_call(
        functools.partial(feed_both_kernel, base, first, piece, own, grads, at, tiles),
        grid=(tiles + 4,),
        in_specs=[SMEM]
        + [ANY] * len(weights)
        + [whole_spec(vectors), whole_spec(bias), tile_spec, tile_spec],
        out_specs=[ANY] * len(grads.out_shapes())
        + [
            tile_spec,
            whole_spec(outs[1]),
            whole_spec(outs[2]),
            pl.BlockSpec((1, 8, 512), lambda i: (jnp.maximum(i - tiles, 0), 0, 0)),
        ],
        out_shape=[far(s) for s in grads.out_shapes()] + outs,
        scratch_shapes=[
            pltpu.VMEM(piece.cut(own), BF),
            pltpu.VMEM(piece.cut(own + 1), BF),
            pltpu.VMEM(grads.cut(at), BF),
            pltpu.VMEM(grads.cut(at + 1), BF),
            pltpu.VMEM((4, tokens, 512), BF),
            pltpu.VMEM((4, tokens, 512), BF),
            pltpu.VMEM((512, tokens), BF),
            pltpu.VMEM((tokens, 512), BF),
            pltpu.SemaphoreType.DMA((2,)),
        ],
        compiler_params=params(44),
        cost_estimate=cost(tokens, 24 * 512 * 512),
        name="feed_both",
    )(me, *weights, vectors, bias, n1, grad)
    m = len(grads.out_shapes())
    return got[:m], got[m], got[m + 1], got[m + 2], got[m + 3][:, 0, :]


def attend_backward_kernel(mode, base, piece, grads, first, shared, *refs):
    refs = list(refs)
    me_ref = refs.pop(0)
    count = piece.refs
    take = lambda k: [refs.pop(0) for _ in range(k)]
    kinds = 3 if mode == "cross" else 2
    weight_refs = [take(count) for _ in range(kinds)]
    vectors_ref, grad_ref, n_ref, inv_ref, q_ref, k_ref, v_ref, o_ref, lse_ref = take(9)
    hot_ref, bar_ref, low_ref = take(3)
    memory_ref = refs.pop(0) if mode == "cross" else None
    lang_ref = refs.pop(0) if mode == "dec" else None
    sum_refs = take(5) if mode == "enc" else None
    cols_ref = refs.pop(0) if mode == "enc" else None
    if shared:
        refs.pop(0)
    grad_outs = take(len(grads.out_shapes()))
    dx_out, sums_out = take(2)
    dm_out = refs.pop(0) if mode == "cross" else None
    lang_out = refs.pop(0) if mode == "dec" else None
    staged_kinds = 2 if mode == "dec" else 3
    weights, staged = take(kinds), take(staged_kinds)
    low_t, o_t, gqs, gks, gvs, gbs, sems = take(7)
    memory_t = refs.pop(0) if mode == "cross" else None
    all_sums = refs.pop(0) if mode == "enc" else None
    step = pl.program_id(0)
    vectors = vectors_ref[...]

    @pl.when(step == 0)
    def _():
        me = me_ref[0]
        for k, (source, dst) in enumerate(zip(weight_refs, weights)):
            piece.fetch(k, me, source, dst, sems.at[k])
        sums_out[...] = jnp.zeros_like(sums_out)
        if mode == "dec":
            lang_out[...] = jnp.zeros_like(lang_out)
        for k, dst in enumerate(weights):
            finish(dst, sems.at[k])

    back, gain, shift = norm_back(
        grad_ref[...], n_ref[...], inv_ref[...], vec(vectors, base + 3)
    )
    gb = back.astype(BF)
    go = dot_t(gb, square(weights[-1], 0)).astype(BF)
    q, k, v, o = q_ref[...], k_ref[...], v_ref[...], o_ref[...]
    gq, gk, gv = heads_backward(go, q, k, v, o, lse_ref[...], hot_ref[...], bar_ref[...])
    if mode == "cross":
        wq, wk, wv = square(weights[0], 0), square(weights[1], 0), square(weights[1], 1)
    else:
        wq, wk, wv = (square(weights[0], j) for j in range(3))
    dx = back + dot_t(gq, wq)
    dm = dot_t(gk, wk) + dot_t(gv, wv)
    if mode == "cross":
        dx_out[...] = dx
        dm_out[...] = dm
    else:
        dx = dx + dm
        dx_out[...] = dx.astype(BF)
    if mode == "dec":
        high = dx.astype(BF)
        rest = (dx - high.astype(F32)).astype(BF)
        hot_lang = lang_ref[...].T
        lang_out[...] += dot(hot_lang, high) + dot(hot_lang, rest)
    sums_out[0:1] += jnp.sum(gq.astype(F32), axis=0, keepdims=True)
    sums_out[1:2] += jnp.sum(gv.astype(F32), axis=0, keepdims=True)
    sums_out[2:3] += jnp.sum(gb.astype(F32), axis=0, keepdims=True)
    sums_out[3:4] += gain[None]
    sums_out[4:5] += shift[None]
    part = pl.ds(pl.multiple_of(step * ROW, ROW), ROW)
    gqs[part], gks[part], gvs[part], gbs[part] = gq, gk, gv, gb
    low_t[:, part] = low_ref[...].T
    o_t[:, part] = o.astype(BF).T
    if mode == "cross":
        memory_t[:, part] = memory_ref[...].T

    @pl.when(step == pl.num_programs(0) - 1)
    def _():
        me = me_ref[0]
        shape = staged[0].shape[1:]
        out_grad = dot(o_t[...], gbs[...]).astype(BF).reshape(shape)
        gq_grad = dot(low_t[...], gqs[...]).astype(BF).reshape(shape)
        kv_t = (memory_t if mode == "cross" else low_t)[...]
        gk_grad = dot(kv_t, gks[...]).astype(BF).reshape(shape)
        gv_grad = dot(kv_t, gvs[...]).astype(BF).reshape(shape)
        if mode == "cross":
            staged[0][0] = gq_grad
            staged[1][0], staged[1][1] = gk_grad, gv_grad
        else:
            staged[0][0], staged[0][1], staged[0][2] = gq_grad, gk_grad, gv_grad
        staged[kinds - 1][0] = out_grad
        if mode == "enc":
            all_sums[...] = jnp.zeros_like(all_sums)
            row = 0
            counts = (8, 5, 3, 5, 5, 3)
            for ref, count in zip([sum_refs[0], sums_out] + sum_refs[1:], counts):
                all_sums[row : row + count] = ref[:count]
                row += count
            block = (all_sums[...].T + cols_ref[...]).astype(BF)
            block = jnp.concatenate([block, jnp.zeros((512, 384), BF)], axis=1)
            staged[2][0] = block.reshape(shape)
        for k, src in enumerate(staged):
            grads.store(first + k, me, src, grad_outs, sems.at[k])
        for k, src in enumerate(staged):
            finish(src, sems.at[k])


def attend_backward(
    mode, base, me, piece, grads, first, vectors, grad, saved, hot, bar, low, extra, fixed=(), into=None
):
    q, k, v, o, lse, n, inv = (near_not(a) for a in saved)
    low = near_not(low)
    extra = [near_not(a) for a in extra]
    grad = grad if mode == "cross" else near_not(grad)
    tokens = hot.shape[0]
    kinds = range(3 if mode == "cross" else 2)
    weights = [a for i in kinds for a in piece.arrays[i]]
    rows = [grad, n, inv, q, k, v, o, lse, hot, bar, low] + list(extra)
    outs = [like(tokens, 512, F32 if mode == "cross" else BF), like(8, 512, F32)]
    out_specs = [row_spec(outs[0]), whole_spec(outs[1])]
    if mode == "cross":
        outs.append(like(tokens, 512, F32))
        out_specs.append(row_spec(outs[-1]))
    if mode == "dec":
        outs.append(like(128, 512, F32))
        out_specs.append(whole_spec(outs[-1]))
    grad_shapes = grads.out_shapes()
    scratch = [pltpu.VMEM(piece.cut(i), BF) for i in kinds]
    scratch += [pltpu.VMEM(grads.cut(first + i), BF) for i in range(2 if mode == "dec" else 3)]
    scratch += [pltpu.VMEM((512, tokens), BF)] * 2 + [pltpu.VMEM((tokens, 512), BF)] * 4
    scratch.append(pltpu.SemaphoreType.DMA((3,)))
    if mode == "cross":
        scratch.append(pltpu.VMEM((512, tokens), BF))
    if mode == "enc":
        scratch.append(pltpu.VMEM((128, 512), F32))
    args = [me, *weights, vectors, *rows, *fixed]
    shared = [] if into is None else [into]
    got = pl.pallas_call(
        functools.partial(attend_backward_kernel, mode, base, piece, grads, first, bool(shared)),
        grid=(tokens // ROW,),
        in_specs=[SMEM]
        + [ANY] * len(weights)
        + [whole_spec(vectors)]
        + [row_spec(a) for a in rows]
        + [whole_spec(a) for a in fixed]
        + [ANY] * len(shared),
        input_output_aliases={len(args): 0} if shared else {},
        out_specs=[ANY] * len(grad_shapes) + out_specs,
        out_shape=[far(s) for s in grad_shapes] + [far(outs[0])] + outs[1:],
        scratch_shapes=scratch,
        compiler_params=params(42),
        cost_estimate=cost(tokens, 8 * 512 * 512 + 5 * 8 * 512 * 256),
        name="attend_backward_" + mode,
    )(*args, *shared)
    m = len(grad_shapes)
    return got[:m], got[m:]


def segment_marks(segments):
    flat = segments.reshape(-1)
    hot = flat[:, None] == jnp.arange(128, dtype=jnp.int32)[None, :]
    bar = jnp.where(~hot & (jnp.arange(128) < 8)[None, :], -BIG, 0.0)
    return hot.astype(BF), bar.astype(BF)


def language_marks(segments, language):
    picked = jnp.zeros_like(segments)
    for s in range(language.shape[1]):
        picked = jnp.where(segments == s, language[:, s : s + 1], picked)
    flat = picked.reshape(-1)
    return (flat[:, None] == jnp.arange(128, dtype=jnp.int32)[None, :]).astype(BF)


def layers(
    grid,
    source,
    target,
    source_segments,
    target_segments,
    target_language,
    cotangent,
    enc_qkv,
    enc_out,
    enc_up,
    enc_down,
    enc_vecs,
    enc_bias_up,
    dec_qkv,
    dec_out,
    cross_q,
    cross_kv,
    cross_out,
    dec_up,
    dec_down,
    dec_vecs,
    dec_bias_up,
    lang_table,
):
    unit = enc_qkv.shape[0]
    feed_forms = [(4, True), (4, False)]
    self_forms = [(3, True), (1, True)]
    cross_forms = [(1, True), (2, True), (1, True)]
    enc_self = Piece(grid, self_forms + [(1, True)])
    dec_self = Piece(grid, self_forms)
    enc_feed = Piece(grid, feed_forms)
    late = Piece(grid, cross_forms + feed_forms, plain=True)
    rows01, rows2, rows3 = pack(
        grid,
        [lang_table, enc_vecs, dec_vecs, enc_bias_up, dec_bias_up],
        [enc_qkv, enc_out, dec_qkv, dec_out],
        [enc_up, enc_down],
        [cross_q, cross_kv, cross_out, dec_up, dec_down],
    )
    held = jnp.stack(z_gather(grid, rows01))
    held0, held1 = held[:, : 5 * unit], held[:, 5 * unit :]
    held2 = z_gather_halves(grid, after(rows2, held1))
    late.arrive(lax.all_gather(rows3, AXES, axis=0, tiled=False))
    held0 = jnp.concatenate(xy_gather(grid, held0), axis=0)
    held0, held2 = after((held0, held2), held1)
    enc_self.arrive(held0, grid.swap_dp(held0, 1))
    held1, held2 = after((held1, held2), held0[0])
    parts1 = xy_gather(grid, held1)
    parts2 = xy_gather_early(grid, held2)

    me = grid.me().astype(jnp.int32).reshape(1)
    source_hot, source_bar = segment_marks(source_segments)
    target_hot, target_bar = segment_marks(target_segments)
    lang = language_marks(target_segments, target_language)

    *enc_saved, vectors, columns = attend_forward(
        "enc", ENC, me, enc_self, 2, (source,), source_hot, source_bar, None
    )
    token = enc_saved[6]
    held1 = jnp.concatenate(after(parts1, token), axis=0)
    dec_self.arrive(held1, grid.swap_dp(held1, 1))
    parts2 = parts2 + xy_gather_rest(grid, after(held2, token))
    enc_bias = columns[:, ENC_UP:DEC_UP].astype(F32).reshape(4, 512)
    dec_bias = columns[:, DEC_UP : DEC_UP + 4].astype(F32).reshape(4, 512)
    *dec_saved, target_low = attend_forward(
        "dec", DEC, me, dec_self, None, (target, lang), target_hot, target_bar, vectors
    )
    held2 = jnp.concatenate(after(parts2, dec_saved[6]), axis=0)
    enc_feed.arrive(held2, grid.swap_dp(held2, 1))
    enc_act, enc_slope, enc_n, enc_inv, encoded = feed_forward(
        ENC + 5, ENC + 3, me, enc_feed, 0, vectors, enc_bias, enc_saved[5]
    )
    *cross_saved, first_low = attend_forward(
        "cross", DEC + 5, me, late, None, (dec_saved[5], encoded), target_hot, source_bar, vectors
    )
    late_back = Piece(grid, cross_forms + feed_forms, plain=True)
    enc_feed_back = Piece(grid, feed_forms)
    dec_back = Piece(grid, self_forms)
    enc_back = Piece(grid, self_forms + [(1, None)])
    outs, dec_output, grad_second, dec_feed_sums, dec_bias_grad = feed_both(
        DEC + 10, DEC + 8, me, late, 3, late_back, 3, vectors, dec_bias, cross_saved[5], cotangent
    )
    shared = outs[0] if grid.tiled else None
    late_outs, (grad_first, cross_sums, grad_encoded) = attend_backward(
        "cross", DEC + 5, me, late, late_back, 0, vectors, grad_second, cross_saved,
        target_hot, source_bar, first_low, (encoded,), into=shared,
    )
    if not grid.tiled:
        late_outs = list(late_outs[:3]) + list(outs[3:])
    late_total = scatter_plain(grid, *late_back.ready(late_outs))

    outs, grad_enc_first, enc_feed_sums, enc_bias_grad = feed_backward(
        ENC + 5, ENC + 3, me, enc_feed, 0, enc_feed_back, 0, vectors, grad_encoded, enc_n, enc_inv,
        enc_saved[5], enc_act, enc_slope,
    )
    keep2, send2 = enc_feed_back.ready(outs)
    got2 = grid.swap_dp(send2, 1)
    grad_first = after(grad_first, enc_feed_sums)
    outs, (target_grad, dec_sums, lang_grad) = attend_backward(
        "dec", DEC, me, dec_self, dec_back, 0, vectors, grad_first, dec_saved,
        target_hot, target_bar, target_low, (lang,),
    )
    keep3, send3 = dec_back.ready(outs)
    got3 = grid.swap_dp(send3, 1)
    got2 = after(got2, dec_sums)
    held2, sends = core_sum(grid, keep2, got2)
    parts2 = xy_scatter(grid, sends)
    cols = jnp.concatenate([enc_bias_grad.reshape(512, 4), dec_bias_grad.reshape(512, 4)], axis=1)
    cols = jnp.pad(cols, ((0, 0), (ENC_UP, 128 - ENC_UP - 8)))
    grad_enc_first = after(grad_enc_first, got2)
    outs, (source_grad, enc_sums) = attend_backward(
        "enc", ENC, me, enc_self, enc_back, 0, vectors, grad_enc_first, enc_saved,
        source_hot, source_bar, source, (), fixed=(lang_grad, enc_feed_sums, dec_sums, cross_sums, dec_feed_sums, cols),
    )
    keep4, send4 = enc_back.ready(outs)
    got4 = grid.swap_dp(send4, 1)
    got3, parts2 = after((got3, parts2), enc_sums)
    held3, sends = core_sum(grid, keep3, got3)
    parts3 = xy_scatter(grid, sends)
    held4, sends = core_sum(grid, keep4, got4)
    parts4 = xy_scatter(grid, sends)

    def last_swaps(*pieces):
        kind = pieces[0][0].dtype
        sends = [
            jnp.concatenate([xy_sum(grid, p, z).astype(kind) for p in pieces])
            for z in range(1, grid.nf)
        ]
        return [grid.swap_fsdp(s, z) for z, s in zip(range(1, grid.nf), sends)]

    all2, all3, all4 = held2 + parts2, held3 + parts3, held4 + parts4
    enc_up_grad, enc_down_grad, dec_qkv_grad, dec_out_grad = shards(
        grid, [enc_feed_back, dec_back], [all2, all3], last_swaps(all2, all3)
    )
    cross_q_grad, cross_kv_grad, cross_out_grad, dec_up_grad, dec_down_grad = shards(
        grid, [late_back], [[late_total[None]]], []
    )
    all4 = after(all4, cross_q_grad)
    enc_qkv_grad, enc_out_grad, *rest = shards(grid, [enc_back], [all4], last_swaps(all4))

    return (
        dec_output,
        source_grad,
        target_grad,
        enc_qkv_grad,
        enc_out_grad,
        enc_up_grad,
        enc_down_grad,
        rest[1],
        rest[3].reshape(-1),
        dec_qkv_grad,
        dec_out_grad,
        cross_q_grad,
        cross_kv_grad,
        cross_out_grad,
        dec_up_grad,
        dec_down_grad,
        rest[2],
        rest[4].reshape(-1),
        rest[0],
    )


def solution(mesh):
    split = P(("dp", "fsdp"))
    return jax.shard_map(
        functools.partial(layers, Grid(mesh)),
        mesh=mesh,
        in_specs=(split,) * 22,
        out_specs=(split,) * 19,
        check_vma=False,
    )
```

profile of v0, /device:TPU:0, one launch (start us, length us, event | category | flops | bytes accessed | tf_op | source)
XLA Modules:
  0.0 348.9 jit_solution(15182979965411226141)
XLA Ops:
  11.9 5.1 %collective-permute-start.2 = (bf16[144,512]{1,0:T(8,128)(2,1)}, bf16[144,512]{1,0:T(8,128)(2,1)S(1)}, u32[]{:S(2)}, u32[]{:S(2)}) collective-permute-start(bf16[144,512]{1,0:T(8,128)(2,1)} %get-tuple-element.117), channel_id=1, source_target_pairs={{0,3},{1,2},{2,1},{3,0},{4,7},{5,6},{6,5},{7,4},{8,11},{9,10},{10,... | collective-permute-start | bytes 442376 | tf_op jit(solution)/shard_map/ppermute | solution.py:44
  17.7 4.3 %collective-permute-done.2 = bf16[144,512]{1,0:T(8,128)(2,1)S(1)} collective-permute-done((bf16[144,512]{1,0:T(8,128)(2,1)}, bf16[144,512]{1,0:T(8,128)(2,1)S(1)}, u32[]{:S(2)}, u32[]{:S(2)}) %collective-permute-start.2) | collective-permute-done | bytes 147488 | tf_op jit(solution)/shard_map/ppermute | solution.py:44
  22.0 10.0 %collective-permute-done.1 = bf16[144,512]{1,0:T(8,128)(2,1)S(1)} collective-permute-done((bf16[144,512]{1,0:T(8,128)(2,1)}, bf16[144,512]{1,0:T(8,128)(2,1)S(1)}, u32[]{:S(2)}, u32[]{:S(2)}) %collective-permute-start.1) | collective-permute-done | bytes 147488 | tf_op jit(solution)/shard_map/ppermute | solution.py:44
  34.0 3.2 collective-permute-start.5
  37.8 3.4 collective-permute-done.6
  41.4 6.0 %collective-permute-done.5 = bf16[4,80,512]{2,1,0:T(8,128)(2,1)S(1)} collective-permute-done((bf16[4,80,512]{2,1,0:T(8,128)(2,1)S(1)}, bf16[4,80,512]{2,1,0:T(8,128)(2,1)S(1)}, u32[]{:S(2)}, u32[]{:S(2)}) %collective-permute-start.5) | collective-permute-done | bytes 327712 | tf_op jit(solution)/shard_map/ppermute | solution.py:41
  47.4 5.3 %collective-permute-done.4 = bf16[4,80,512]{2,1,0:T(8,128)(2,1)S(1)} collective-permute-done((bf16[4,80,512]{2,1,0:T(8,128)(2,1)S(1)}, bf16[4,80,512]{2,1,0:T(8,128)(2,1)S(1)}, u32[]{:S(2)}, u32[]{:S(2)}) %collective-permute-start.4) | collective-permute-done | bytes 327712 | tf_op jit(solution)/shard_map/ppermute | solution.py:41
  52.7 2.9 collective-permute-done.3
  60.2 13.7 %attend_forward_enc.1 = (bf16[1024,512]{1,0:T(8,128)(2,1)}, bf16[1024,512]{1,0:T(8,128)(2,1)}, bf16[1024,512]{1,0:T(8,128)(2,1)}, f32[1024,512]{1,0:T(8,128)}, f...) custom-call(s32[1]{0:T(128)} %bitcast.refs_0_, ...), custom_call_target="tpu_custom_call" | custom-call | flops 6442450944 | bytes 8388608 | tf_op jit(solution)/shard_map/attend_forward_enc/pallas_call | solution.py:641
  73.9 2.2 collective-permute-done.10
  77.9 2.2 collective-permute-start.13
  81.7 13.2 %attend_forward_dec.1 = (bf16[1024,512]{1,0:T(8,128)(2,1)}, bf16[1024,512]{1,0:T(8,128)(2,1)}, bf16[1024,512]{1,0:T(8,128)(2,1)}, f32[1024,512]{1,0:T(8,128)}, f...) custom-call(s32[1]{0:T(128)} %bitcast.refs_0_, ...), custom_call_target="tpu_custom_call" | custom-call | flops 6442450944 | bytes 8388608 | tf_op jit(solution)/shard_map/attend_forward_dec/pallas_call | solution.py:641
  94.9 10.7 %collective-permute-done.15 = bf16[4,128,512]{2,1,0:T(8,128)(2,1)S(1)} collective-permute-done((bf16[4,128,512]{2,1,0:T(8,128)(2,1)S(1)}, bf16[4,128,512]{2,1,0:T(8,128)(2,1)S(1)}, u32[]{:S(2)}, u32[]{:S(2)}) %collective-permute-start.15) | collective-permute-done | bytes 524320 | tf_op jit(solution)/shard_map/ppermute | solution.py:41
  109.5 4.0 %collective-permute-done.16 = bf16[16,128,512]{2,1,0:T(8,128)(2,1)} collective-permute-done((bf16[16,128,512]{2,1,0:T(8,128)(2,1)}, bf16[16,128,512]{2,1,0:T(8,128)(2,1)}, u32[]{:S(2)}, u32[]{:S(2)}) %collective-permute-start.16) | collective-permute-done | bytes 2097184 | tf_op jit(solution)/shard_map/ppermute | solution.py:41
  113.5 14.6 %feed_forward.1 = (bf16[4,1024,512]{2,1,0:T(8,128)(2,1)}, bf16[4,1024,512]{2,1,0:T(8,128)(2,1)}, f32[1024,512]{1,0:T(8,128)}, f32[1024,1]{1,0:T(8,128)}, bf16[1024,512]{1,0:T(8,128)(2,1)S(1)}) custom-call(s32[1]{0:T(128)} %bitcast.refs_0_, bf16[16,8,16,512]{3,2,1,0:T(8,128)(2,1)} %bitcast.13.refs_1_.refs_3_, ...), custom_call_target="tpu_custom_call" | custom-call | flops 4294967296 | bytes 8388608 | tf_op jit(solution)/shard_map/feed_forward/pallas_call | solution.py:710
  128.2 13.4 %attend_forward_cross.1 = (bf16[1024,512]{1,0:T(8,128)(2,1)}, bf16[1024,512]{1,0:T(8,128)(2,1)}, bf16[1024,512]{1,0:T(8,128)(2,1)}, f32[1024,512]{1,0:T(8,128)},...) custom-call(s32[1]{0:T(128)} %bitcast.refs_0_, ...), custom_call_target="tpu_custom_call" | custom-call | flops 6442450944 | bytes 8388608 | tf_op jit(solution)/shard_map/attend_forward_cross/pallas_call | solution.py:641
  141.7 25.2 %feed_both.1 = (bf16[32,12,16,512]{3,2,1,0:T(8,128)(2,1)}, bf16[1024,512]{1,0:T(8,128)(2,1)}, f32[1024,512]{1,0:T(8,128)S(1)}, f32[8,512]{1,0:T(8,128)S(1)}, f32[4,8,512]{2,1,0:T(8,128)S(1)}) custom-call(s32[1]{0:T(128)} %bitcast.refs_0_, bf16[32,12,16,512]{3,2,1,0:T(8,128)(2,1)} %bitcast.211, bf16[32,12,16,512]{3,2,1,0:T(8,128)(2,1)} %bitcast.212, ...), custom_call_target="tpu_custom_call" | custom-call | flops 12884901888 | bytes 8388608 | tf_op jit(solution)/shard_map/feed_both/pallas_call | solution.py:903
  166.9 26.0 %attend_backward_cross.1 = (bf16[32,12,16,512]{3,2,1,0:T(8,128)(2,1)}, f32[1024,512]{1,0:T(8,128)}, f32[8,512]{1,0:T(8,128)S(1)}, f32[1024,512]{1,0:T(8,128)S(1)}) custom-call(s32[1]{0:T(128)} %bitcast.refs_0_, bf16[32,12,16,512]{3,2,1,0:T(8,128)(2,1)} %bitcast.213, bf16[32,12,16,512]{3,2,1,0:T(8,128)(2,1)} %bitcast.214, ...), custom_call_target="tpu_custom_call", output_to_operand_aliasing={{0}: (17, {})} | custom-call | flops 15032385536 | bytes 8388608 | tf_op jit(solution)/shard_map/attend_backward_cross/pallas_call | solution.py:1071
  195.9 18.7 %feed_backward.1 = (bf16[16,8,16,512]{3,2,1,0:T(8,128)(2,1)}, bf16[16,8,16,512]{3,2,1,0:T(8,128)(2,1)}, f32[1024,512]{1,0:T(8,128)}, f32[8,512]{1,0:T(8,128)S(1)}, f32[4,8,512]{2,1,0:T(8,128)S(1)}) custom-call(s32[1]{0:T(128)} %bitcast.refs_0_, bf16[16,8,16,512]{3,2,1,0:T(8,128)(2,1)} %bitcast.13.refs_1_.refs_3_, ...), custom_call_target="tpu_custom_call" | custom-call | flops 8589934592 | bytes 8388608 | tf_op jit(solution)/shard_map/feed_backward/pallas_call | solution.py:794
  215.5 29.6 %attend_backward_dec.1 = (bf16[16,4,16,512]{3,2,1,0:T(8,128)(2,1)}, bf16[16,4,16,512]{3,2,1,0:T(8,128)(2,1)}, bf16[1024,512]{1,0:T(8,128)(2,1)}, f32[8,512]{1,0:T(8,128)S(1)}, f32[128,512]{1,0:T(8,128)S(1)}) custom-call(s32[1]{0:T(128)} %bitcast.refs_0_, bf16[16,4,16,512]{3,2,1,0:T(8,128)(2,1)} %bitcast.197, bf16[16,4,16,512]{3,2,1,0:T(8,128)(2,1)} %bitcast.220, ...), custom_call_target="tpu_custom_call" | custom-call | flops 15032385536 | bytes 8388608 | tf_op jit(solution)/shard_map/attend_backward_dec/pallas_call | solution.py:1071
  252.9 28.9 %attend_backward_enc.1 = (bf16[16,5,16,512]{3,2,1,0:T(8,128)(2,1)}, bf16[16,5,16,512]{3,2,1,0:T(8,128)(2,1)}, bf16[1024,512]{1,0:T(8,128)(2,1)}, f32[8,512]{1,0:T(8,128)}) custom-call(s32[1]{0:T(128)} %bitcast.refs_0_, bf16[16,5,16,512]{3,2,1,0:T(8,128)(2,1)} %bitcast.180, bf16[16,5,16,512]{3,2,1,0:T(8,128)(2,1)} %bitcast.10.refs_2_.refs_4_.refs_6_, ...), custom_call_target="tpu_custom_call" | custom-call | flops 15032385536 | bytes 8388608 | tf_op jit(solution)/shard_map/attend_backward_enc/pallas_call | solution.py:1071
  288.9 5.0 %collective-permute-done.31.refs_9_ = bf16[4,64,512]{2,1,0:T(8,128)(2,1)S(1)} collective-permute-done((bf16[4,64,512]{2,1,0:T(8,128)(2,1)S(1)}, bf16[4,64,512]{2,1,0:T(8,128)(2,1)S(1)}, u32[]{:S(2)}, u32[]{:S(2)}) %collective-permute-start.31) | collective-permute-done | bytes 262176 | tf_op jit(solution)/shard_map/ppermute | solution.py:41
  293.9 5.2 %collective-permute-done.30.refs_8_ = bf16[4,64,512]{2,1,0:T(8,128)(2,1)S(1)} collective-permute-done((bf16[4,64,512]{2,1,0:T(8,128)(2,1)S(1)}, bf16[4,64,512]{2,1,0:T(8,128)(2,1)S(1)}, u32[]{:S(2)}, u32[]{:S(2)}) %collective-permute-start.30) | collective-permute-done | bytes 262176 | tf_op jit(solution)/shard_map/ppermute | solution.py:41
  299.3 2.2 fusion.3
  305.7 3.2 collective-permute-start.32
  313.2 2.7 collective-permute-start.34
  315.9 3.4 collective-permute-done.20.refs_3_
  319.5 2.6 collective-permute-start.24
  322.1 2.2 collective-permute-start.23
  326.9 2.7 collective-permute-done.33.refs_11_
  330.3 2.3 shards.5
  332.7 3.5 %collective-permute-done.23.refs_6_ = bf16[80,512]{1,0:T(8,128)(2,1)S(1)} collective-permute-done((bf16[80,512]{1,0:T(8,128)(2,1)S(1)}, bf16[80,512]{1,0:T(8,128)(2,1)S(1)}, u32[]{:S(2)}, u32[]{:S(2)}) %collective-permute-start.23) | collective-permute-done | bytes 81952 | tf_op jit(solution)/shard_map/ppermute | solution.py:44
  (186 shorter events, 56.4 us)
Async XLA Ops:
  7.2 121.0 %all-gather.3.cloned.1.call-start = ((), (), s32[]{:S(2)}) async-start(), calls=%async_computation.4 | async-start | bytes 6488064 | tf_op jit(solution)/shard_map/all_gather | solution.py:1150
  11.9 271.5 %reduce-scatter.3.cloned.1.call-start = ((), (), s32[]{:S(2)}) async-start(), calls=%async_computation.2 | async-start | bytes 7077888 | tf_op jit(solution)/shard_map/reduce_scatter | solution.py:200
  17.1 14.9 %collective-permute-start.1 = (bf16[144,512]{1,0:T(8,128)(2,1)}, bf16[144,512]{1,0:T(8,128)(2,1)S(1)}, u32[]{:S(2)}, u32[]{:S(2)}) collective-permute-start(bf16[144,512]{1,0:T(8,128)(2,1)} %get-tuple-element.117), channel_id=1, source_target_pairs={{0,2},{1,3},{2,0},{3,1},{4,6},{5,7},{6,4},{7,5},{8,10},{9,11},{10,... | collective-permute-start | bytes 442376 | tf_op jit(solution)/shard_map/ppermute | solution.py:44
  17.1 14.9 %collective-permute-start = (bf16[144,512]{1,0:T(8,128)(2,1)}, bf16[144,512]{1,0:T(8,128)(2,1)S(1)}, u32[]{:S(2)}, u32[]{:S(2)}) collective-permute-start(bf16[144,512]{1,0:T(8,128)(2,1)} %get-tuple-element.117), channel_id=1, source_target_pairs={{0,1},{1,0},{2,3},{3,2},{4,5},{5,4},{6,7},{7,6},{8,9},{9,8},{10,11... | collective-permute-start | bytes 442376 | tf_op jit(solution)/shard_map/ppermute | solution.py:44
  34.0 13.4 %collective-permute-start.5 = (bf16[4,80,512]{2,1,0:T(8,128)(2,1)S(1)}, bf16[4,80,512]{2,1,0:T(8,128)(2,1)S(1)}, u32[]{:S(2)}, u32[]{:S(2)}) collective-permute-start(bf16[4,80,512]{2,1,0:T(8,128)(2,1)S(1)} %slice.383), channel_id=1, source_target_pairs={{0,24},{4,28},{8,16},{12,20},{16,8},{20,12},{24,0},{28,4},{1,25},{... | collective-permute-start | bytes 983048 | tf_op jit(solution)/shard_map/ppermute | solution.py:41
  37.1 15.6 %collective-permute-start.4 = (bf16[4,80,512]{2,1,0:T(8,128)(2,1)S(1)}, bf16[4,80,512]{2,1,0:T(8,128)(2,1)S(1)}, u32[]{:S(2)}, u32[]{:S(2)}) collective-permute-start(bf16[4,80,512]{2,1,0:T(8,128)(2,1)S(1)} %slice.383), channel_id=1, source_target_pairs={{0,16},{4,20},{8,24},{12,28},{16,0},{20,4},{24,8},{28,12},{1,17},{... | collective-permute-start | bytes 983048 | tf_op jit(solution)/shard_map/ppermute | solution.py:41
  37.1 18.5 %collective-permute-start.3 = (bf16[4,80,512]{2,1,0:T(8,128)(2,1)S(1)}, bf16[4,80,512]{2,1,0:T(8,128)(2,1)S(1)}, u32[]{:S(2)}, u32[]{:S(2)}) collective-permute-start(bf16[4,80,512]{2,1,0:T(8,128)(2,1)S(1)} %slice.383), channel_id=1, source_target_pairs={{0,8},{4,12},{8,0},{12,4},{16,24},{20,28},{24,16},{28,20},{1,9},{5... | collective-permute-start | bytes 983048 | tf_op jit(solution)/shard_map/ppermute | solution.py:41
  41.2 14.6 %collective-permute-start.7 = (bf16[2,128,512]{2,1,0:T(8,128)(2,1)S(1)}, bf16[2,128,512]{2,1,0:T(8,128)(2,1)S(1)}, u32[]{:S(2)}, u32[]{:S(2)}) collective-permute-start(bf16[2,128,512]{2,1,0:T(8,128)(2,1)S(1)} %pad_maximum_fusion.4), channel_id=1, source_target_pairs={{0,1},{1,0},{2,3},{3,2},{4,5},{5,4},{6,7},{7,6},{8,9},{9,8},{10,11... | collective-permute-start | bytes 786440 | tf_op jit(solution)/shard_map/ppermute | solution.py:44
  56.6 17.3 %collective-permute-start.11 = (bf16[4,64,512]{2,1,0:T(8,128)(2,1)S(1)}, bf16[4,64,512]{2,1,0:T(8,128)(2,1)S(1)}, u32[]{:S(2)}, u32[]{:S(2)}) collective-permute-start(bf16[4,64,512]{2,1,0:T(8,128)(2,1)S(1)} %pad_maximum_fusion.3), channel_id=1, source_target_pairs={{0,24},{4,28},{8,16},{12,20},{16,8},{20,12},{24,0},{28,4},{1,25},{... | collective-permute-start | bytes 786440 | tf_op jit(solution)/shard_map/ppermute | solution.py:41
  58.1 18.0 %collective-permute-start.10 = (bf16[4,64,512]{2,1,0:T(8,128)(2,1)S(1)}, bf16[4,64,512]{2,1,0:T(8,128)(2,1)S(1)}, u32[]{:S(2)}, u32[]{:S(2)}) collective-permute-start(bf16[4,64,512]{2,1,0:T(8,128)(2,1)S(1)} %pad_maximum_fusion.3), channel_id=1, source_target_pairs={{0,16},{4,20},{8,24},{12,28},{16,0},{20,4},{24,8},{28,12},{1,17},{... | collective-permute-start | bytes 786440 | tf_op jit(solution)/shard_map/ppermute | solution.py:41
  59.8 16.4 %collective-permute-start.9 = (bf16[4,64,512]{2,1,0:T(8,128)(2,1)S(1)}, bf16[4,64,512]{2,1,0:T(8,128)(2,1)S(1)}, u32[]{:S(2)}, u32[]{:S(2)}) collective-permute-start(bf16[4,64,512]{2,1,0:T(8,128)(2,1)S(1)} %pad_maximum_fusion.3), channel_id=1, source_target_pairs={{0,8},{4,12},{8,0},{12,4},{16,24},{20,28},{24,16},{28,20},{1,9},{5... | collective-permute-start | bytes 786440 | tf_op jit(solution)/shard_map/ppermute | solution.py:41
  77.2 17.8 %collective-permute-start.14 = (bf16[4,128,512]{2,1,0:T(8,128)(2,1)S(1)}, bf16[4,128,512]{2,1,0:T(8,128)(2,1)S(1)}, u32[]{:S(2)}, u32[]{:S(2)}) collective-permute-start(bf16[4,128,512]{2,1,0:T(8,128)(2,1)S(1)} %pad_maximum_fusion.2), channel_id=1, source_target_pairs={{0,16},{4,20},{8,24},{12,28},{16,0},{20,4},{24,8},{28,12},{1,17},{... | collective-permute-start | bytes 1572872 | tf_op jit(solution)/shard_map/ppermute | solution.py:41
  77.9 17.0 %collective-permute-start.13 = (bf16[4,128,512]{2,1,0:T(8,128)(2,1)S(1)}, bf16[4,128,512]{2,1,0:T(8,128)(2,1)S(1)}, u32[]{:S(2)}, u32[]{:S(2)}) collective-permute-start(bf16[4,128,512]{2,1,0:T(8,128)(2,1)S(1)} %pad_maximum_fusion.2), channel_id=1, source_target_pairs={{0,8},{4,12},{8,0},{12,4},{16,24},{20,28},{24,16},{28,20},{1,9},{5... | collective-permute-start | bytes 1572872 | tf_op jit(solution)/shard_map/ppermute | solution.py:41
  80.1 25.6 %collective-permute-start.15 = (bf16[4,128,512]{2,1,0:T(8,128)(2,1)S(1)}, bf16[4,128,512]{2,1,0:T(8,128)(2,1)S(1)}, u32[]{:S(2)}, u32[]{:S(2)}) collective-permute-start(bf16[4,128,512]{2,1,0:T(8,128)(2,1)S(1)} %pad_maximum_fusion.2), channel_id=1, source_target_pairs={{0,24},{4,28},{8,16},{12,20},{16,8},{20,12},{24,0},{28,4},{1,25},{... | collective-permute-start | bytes 1572872 | tf_op jit(solution)/shard_map/ppermute | solution.py:41
  194.3 117.1 %reduce-scatter.5.cloned.1.call-start = ((), (), s32[]{:S(2)}) async-start(), calls=%async_computation.3 | async-start | bytes 983040 | tf_op jit(solution)/shard_map/reduce_scatter | solution.py:203
  214.6 32.9 %collective-permute-start.17 = (bf16[16,128,512]{2,1,0:T(8,128)(2,1)}, bf16[16,128,512]{2,1,0:T(8,128)(2,1)}, u32[]{:S(2)}, u32[]{:S(2)}) collective-permute-start(bf16[16,128,512]{2,1,0:T(8,128)(2,1)} %bitcast.216), channel_id=1, source_target_pairs={{0,4},{4,0},{8,12},{12,8},{16,20},{20,16},{24,28},{28,24},{1,5},{5... | collective-permute-start | bytes 6291464 | tf_op jit(solution)/shard_map/ppermute | solution.py:41
  245.1 38.3 %collective-permute-start.25 = (bf16[16,64,512]{2,1,0:T(8,128)(2,1)}, bf16[16,64,512]{2,1,0:T(8,128)(2,1)S(1)}, u32[]{:S(2)}, u32[]{:S(2)}) collective-permute-start(bf16[16,64,512]{2,1,0:T(8,128)(2,1)} %bitcast.222), channel_id=1, source_target_pairs={{0,4},{4,0},{8,12},{12,8},{16,20},{20,16},{24,28},{28,24},{1,5},{5... | collective-permute-start | bytes 3145736 | tf_op jit(solution)/shard_map/ppermute | solution.py:41
  249.3 34.0 %collective-permute-start.28 = (bf16[4,128,512]{2,1,0:T(8,128)(2,1)S(1)}, bf16[4,128,512]{2,1,0:T(8,128)(2,1)S(1)}, u32[]{:S(2)}, u32[]{:S(2)}) collective-permute-start(bf16[4,128,512]{2,1,0:T(8,128)(2,1)S(1)} %get-tuple-element.303), channel_id=1, source_target_pairs={{0,24},{4,28},{8,16},{12,20},{16,8},{20,12},{24,0},{28,4},{1,25},{... | collective-permute-start | bytes 1572872 | tf_op jit(solution)/shard_map/ppermute | solution.py:41
  250.5 32.8 %collective-permute-start.27 = (bf16[4,128,512]{2,1,0:T(8,128)(2,1)S(1)}, bf16[4,128,512]{2,1,0:T(8,128)(2,1)S(1)}, u32[]{:S(2)}, u32[]{:S(2)}) collective-permute-start(bf16[4,128,512]{2,1,0:T(8,128)(2,1)S(1)} %get-tuple-element.304), channel_id=1, source_target_pairs={{0,16},{4,20},{8,24},{12,28},{16,0},{20,4},{24,8},{28,12},{1,17},{... | collective-permute-start | bytes 1572872 | tf_op jit(solution)/shard_map/ppermute | solution.py:41
  252.6 30.8 %collective-permute-start.26 = (bf16[4,128,512]{2,1,0:T(8,128)(2,1)S(1)}, bf16[4,128,512]{2,1,0:T(8,128)(2,1)S(1)}, u32[]{:S(2)}, u32[]{:S(2)}) collective-permute-start(bf16[4,128,512]{2,1,0:T(8,128)(2,1)S(1)} %get-tuple-element.305), channel_id=1, source_target_pairs={{0,8},{4,12},{8,0},{12,4},{16,24},{20,28},{24,16},{28,20},{1,9},{5... | collective-permute-start | bytes 1572872 | tf_op jit(solution)/shard_map/ppermute | solution.py:41
  281.8 17.5 %collective-permute-start.18 = (bf16[16,80,512]{2,1,0:T(8,128)(2,1)}, bf16[16,80,512]{2,1,0:T(8,128)(2,1)}, u32[]{:S(2)}, u32[]{:S(2)}) collective-permute-start(bf16[16,80,512]{2,1,0:T(8,128)(2,1)} %bitcast.217), channel_id=1, source_target_pairs={{0,4},{4,0},{8,12},{12,8},{16,20},{20,16},{24,28},{28,24},{1,5},{5... | collective-permute-start | bytes 3932168 | tf_op jit(solution)/shard_map/ppermute | solution.py:41
  285.0 14.1 %collective-permute-start.30 = (bf16[4,64,512]{2,1,0:T(8,128)(2,1)S(1)}, bf16[4,64,512]{2,1,0:T(8,128)(2,1)S(1)}, u32[]{:S(2)}, u32[]{:S(2)}) collective-permute-start(bf16[4,64,512]{2,1,0:T(8,128)(2,1)S(1)} %get-tuple-element.327), channel_id=1, source_target_pairs={{0,16},{4,20},{8,24},{12,28},{16,0},{20,4},{24,8},{28,12},{1,17},{... | collective-permute-start | bytes 786440 | tf_op jit(solution)/shard_map/ppermute | solution.py:41
  287.0 12.1 %collective-permute-start.29 = (bf16[4,64,512]{2,1,0:T(8,128)(2,1)S(1)}, bf16[4,64,512]{2,1,0:T(8,128)(2,1)S(1)}, u32[]{:S(2)}, u32[]{:S(2)}) collective-permute-start(bf16[4,64,512]{2,1,0:T(8,128)(2,1)S(1)} %get-tuple-element.328), channel_id=1, source_target_pairs={{0,8},{4,12},{8,0},{12,4},{16,24},{20,28},{24,16},{28,20},{1,9},{5... | collective-permute-start | bytes 786440 | tf_op jit(solution)/shard_map/ppermute | solution.py:41
  301.5 11.7 %collective-permute-start.21 = (bf16[4,80,512]{2,1,0:T(8,128)(2,1)}, bf16[4,80,512]{2,1,0:T(8,128)(2,1)S(1)}, u32[]{:S(2)}, u32[]{:S(2)}) collective-permute-start(bf16[4,80,512]{2,1,0:T(8,128)(2,1)} %get-tuple-element.316), channel_id=1, source_target_pairs={{0,24},{4,28},{8,16},{12,20},{16,8},{20,12},{24,0},{28,4},{1,25},{... | collective-permute-start | bytes 983048 | tf_op jit(solution)/shard_map/ppermute | solution.py:41
  303.2 16.2 %collective-permute-start.20 = (bf16[4,80,512]{2,1,0:T(8,128)(2,1)S(1)}, bf16[4,80,512]{2,1,0:T(8,128)(2,1)S(1)}, u32[]{:S(2)}, u32[]{:S(2)}) collective-permute-start(bf16[4,80,512]{2,1,0:T(8,128)(2,1)S(1)} %get-tuple-element.317), channel_id=1, source_target_pairs={{0,16},{4,20},{8,24},{12,28},{16,0},{20,4},{24,8},{28,12},{1,17},{... | collective-permute-start | bytes 983048 | tf_op jit(solution)/shard_map/ppermute | solution.py:41
  303.8 15.6 %collective-permute-start.19 = (bf16[4,80,512]{2,1,0:T(8,128)(2,1)S(1)}, bf16[4,80,512]{2,1,0:T(8,128)(2,1)S(1)}, u32[]{:S(2)}, u32[]{:S(2)}) collective-permute-start(bf16[4,80,512]{2,1,0:T(8,128)(2,1)S(1)} %get-tuple-element.318), channel_id=1, source_target_pairs={{0,8},{4,12},{8,0},{12,4},{16,24},{20,28},{24,16},{28,20},{1,9},{5... | collective-permute-start | bytes 983048 | tf_op jit(solution)/shard_map/ppermute | solution.py:41
  305.7 18.7 %collective-permute-start.32 = (bf16[192,512]{1,0:T(8,128)(2,1)}, bf16[192,512]{1,0:T(8,128)(2,1)}, u32[]{:S(2)}, u32[]{:S(2)}) collective-permute-start(bf16[192,512]{1,0:T(8,128)(2,1)} %pad_maximum_fusion.5), channel_id=1, source_target_pairs={{0,1},{1,0},{2,3},{3,2},{4,5},{5,4},{6,7},{7,6},{8,9},{9,8},{10,11... | collective-permute-start | bytes 589832 | tf_op jit(solution)/shard_map/ppermute | solution.py:44
  309.6 20.1 %collective-permute-start.33 = (bf16[192,512]{1,0:T(8,128)(2,1)}, bf16[192,512]{1,0:T(8,128)(2,1)}, u32[]{:S(2)}, u32[]{:S(2)}) collective-permute-start(bf16[192,512]{1,0:T(8,128)(2,1)} %pad_maximum_fusion.6), channel_id=1, source_target_pairs={{0,2},{1,3},{2,0},{3,1},{4,6},{5,7},{6,4},{7,5},{8,10},{9,11},{10,... | collective-permute-start | bytes 589832 | tf_op jit(solution)/shard_map/ppermute | solution.py:44
  313.2 16.5 %collective-permute-start.34 = (bf16[192,512]{1,0:T(8,128)(2,1)}, bf16[192,512]{1,0:T(8,128)(2,1)S(1)}, u32[]{:S(2)}, u32[]{:S(2)}) collective-permute-start(bf16[192,512]{1,0:T(8,128)(2,1)} %pad_maximum_fusion.7), channel_id=1, source_target_pairs={{0,3},{1,2},{2,1},{3,0},{4,7},{5,6},{6,5},{7,4},{8,11},{9,10},{10,... | collective-permute-start | bytes 589832 | tf_op jit(solution)/shard_map/ppermute | solution.py:44
  319.5 13.1 %collective-permute-start.24 = (bf16[80,512]{1,0:T(8,128)(2,1)S(1)}, bf16[80,512]{1,0:T(8,128)(2,1)S(1)}, u32[]{:S(2)}, u32[]{:S(2)}) collective-permute-start(bf16[80,512]{1,0:T(8,128)(2,1)S(1)} %get-tuple-element.313), channel_id=1, source_target_pairs={{0,3},{1,2},{2,1},{3,0},{4,7},{5,6},{6,5},{7,4},{8,11},{9,10},{10,... | collective-permute-start | bytes 245768 | tf_op jit(solution)/shard_map/ppermute | solution.py:44
  322.1 14.1 %collective-permute-start.23 = (bf16[80,512]{1,0:T(8,128)(2,1)S(1)}, bf16[80,512]{1,0:T(8,128)(2,1)S(1)}, u32[]{:S(2)}, u32[]{:S(2)}) collective-permute-start(bf16[80,512]{1,0:T(8,128)(2,1)S(1)} %get-tuple-element.314), channel_id=1, source_target_pairs={{0,2},{1,3},{2,0},{3,1},{4,6},{5,7},{6,4},{7,5},{8,10},{9,11},{10,... | collective-permute-start | bytes 245768 | tf_op jit(solution)/shard_map/ppermute | solution.py:44
  324.3 11.9 %collective-permute-start.22 = (bf16[80,512]{1,0:T(8,128)(2,1)S(1)}, bf16[80,512]{1,0:T(8,128)(2,1)S(1)}, u32[]{:S(2)}, u32[]{:S(2)}) collective-permute-start(bf16[80,512]{1,0:T(8,128)(2,1)S(1)} %get-tuple-element.315), channel_id=1, source_target_pairs={{0,1},{1,0},{2,3},{3,2},{4,5},{5,4},{6,7},{7,6},{8,9},{9,8},{10,11... | collective-permute-start | bytes 245768 | tf_op jit(solution)/shard_map/ppermute | solution.py:44
  (42 other events, 419.8 us)
Sparse Core Ops, SparseCore 0:
  12.0 84.6 all-gather.2
  194.4 74.6 reduce-scatter.2
  283.6 23.4 reduce-scatter.4
where the time goes:
time: 352 us; the launch traced here: 349 us
  Pallas kernels  191 us (54%)
  waiting for transfers between devices  68.9 us (20%)
  starting transfers between devices  39.3 us (11%)
  local copies, waits for them, and re-layouts  23.1 us (7%)
  between operations  14.8 us (4%)
  other arithmetic  11.5 us (3%)
    pallas_call x3, Pallas kernels, attend_backward(): pl.pallas_call(functools.partial(attend_backward_kernel, mode, base, piec...  84.5 us
    ppermute x24, waiting for transfers between devices, swap_dp(): return lax.ppermute(value, 'dp', [(i, i ^ flip) for i in range(self.nd)])  44.9 us
    pallas_call x3, Pallas kernels, attend_forward(): pl.pallas_call(functools.partial(attend_forward_kernel, mode, base, piece...  40.4 us
    pallas_call x1, Pallas kernels, feed_both(): pl.pallas_call(functools.partial(feed_both_kernel, base, first, piece, ow...  25.2 us
    ppermute x11, waiting for transfers between devices, swap_fsdp(): return lax.ppermute(value, 'fsdp', [(i, i ^ flip) for i in range(self.nf)])  23.9 us
    ppermute x24, starting transfers between devices, swap_dp(): return lax.ppermute(value, 'dp', [(i, i ^ flip) for i in range(self.nd)])  22.4 us
    pallas_call x1, Pallas kernels, feed_backward(): pl.pallas_call(functools.partial(feed_backward_kernel, base, first, piece...  18.7 us
    ppermute x11, starting transfers between devices, swap_fsdp(): return lax.ppermute(value, 'fsdp', [(i, i ^ flip) for i in range(self.nf)])  16.8 us
  transfers between devices with their start and end apart: 38, of which 14 were waited for; matrix products, arithmetic and copies ran while one was open for 7% of the time, Pallas kernels for 35%

commit v1 on v0

--- a/solution.py
+++ b/solution.py
@@ -450,7 +450,7 @@
             tops.append(top)
         sums = total[:, 128:]
         outs.append(total[:, :128] / sums)
-        logs.append(jnp.where(lanes() < HALF, tops[0], tops[1]) + jnp.log(sums))
+        logs.append(minus_parts(jnp.where(lanes() < HALF, tops[0], tops[1]) + jnp.log(sums)))
     return jnp.concatenate(outs, axis=1), jnp.concatenate(logs, axis=1)
 
 
@@ -467,7 +467,7 @@
         high = prod.astype(jnp.bfloat16)
         low = (prod - high.astype(jnp.float32)).astype(jnp.bfloat16)
         delta = dot(jnp.concatenate([high, low], axis=1), same)
-        qa = jnp.concatenate([qs, hot + minus_parts(pair(lse, p))], axis=1)
+        qa = jnp.concatenate([qs, hot + pair(lse, p)], axis=1)
         ga = jnp.concatenate([gp, minus_parts(delta)], axis=1)
         gq = gk = gv = None
         for h in (0, 1):
@@ -571,15 +571,16 @@
     @pl.when(pl.program_id(0) == 0)
     def _():
         me = me_ref[0]
+        if small is not None:
+            piece.fetch(small, me, small_refs, small_scr, sems.at[3])
         for k, (source, dst) in enumerate(zip(proj_refs, weights)):
             piece.fetch(k, me, source, dst, sems.at[k])
         if small is not None:
-            piece.fetch(small, me, small_refs, small_scr, sems.at[3])
             finish(small_scr, sems.at[3])
             block = small_scr[0].reshape(512, 512)[:, :128]
             small_out[...] = block
             vectors_out[...] = block.astype(F32).T
-        for k, dst in enumerate(weights):
+        for k, dst in enumerate(weights[:-1]):
             finish(dst, sems.at[k])
 
     vectors = (vectors_out if small is not None else vectors_ref)[...]
@@ -606,6 +607,11 @@
     q_out[...], k_out[...], v_out[...] = q, k, v
     o, lse = heads_forward(q, k, v, hot_ref[...], bar_ref[...])
     o_out[...], lse_out[...] = o, lse
+
+    @pl.when(pl.program_id(0) == 0)
+    def _():
+        finish(out_w, sems.at[len(weights) - 1])
+
     branch = dot(o.astype(BF), square(out_w, 0)) + vec(vectors, base + 2)
     n_out[...], inv_out[...] = norm(residual + branch)
 
@@ -626,7 +632,8 @@
     rows = [near_not(inputs[0])] + list(inputs[1:]) + [hot, bar]
     args += rows
     specs += [row_spec(a) for a in rows]
-    outs = [like(tokens, 512, BF)] * 3 + [like(tokens, 512, F32)] * 3 + [like(tokens, 1, F32)]
+    outs = [like(tokens, 512, BF)] * 3 + [like(tokens, 512, F32), like(tokens, 512, BF)]
+    outs += [like(tokens, 512, F32), like(tokens, 1, F32)]
     if mode != "enc":
         outs.append(like(tokens, 512, BF))
     out_specs = [row_spec(o) for o in outs]
@@ -968,13 +975,17 @@
         sums_out[...] = jnp.zeros_like(sums_out)
         if mode == "dec":
             lang_out[...] = jnp.zeros_like(lang_out)
+
+    back, gain, shift = norm_back(
+        grad_ref[...], n_ref[...], inv_ref[...], vec(vectors, base + 3)
+    )
+    gb = back.astype(BF)
+
+    @pl.when(step == 0)
+    def _():
         for k, dst in enumerate(weights):
             finish(dst, sems.at[k])
 
-    back, gain, shift = norm_back(
-        grad_ref[...], n_ref[...], inv_ref[...], vec(vectors, base + 3)
-    )
-    gb = back.astype(BF)
     go = dot_t(gb, square(weights[-1], 0)).astype(BF)
     q, k, v, o = q_ref[...], k_ref[...], v_ref[...], o_ref[...]
     gq, gk, gv = heads_backward(go, q, k, v, o, lse_ref[...], hot_ref[...], bar_ref[...])
@@ -1220,11 +1231,12 @@
         source_hot, source_bar, source, (), fixed=(lang_grad, enc_feed_sums, dec_sums, cross_sums, dec_feed_sums, cols),
     )
     keep4, send4 = enc_back.ready(outs)
-    got4 = grid.swap_dp(send4, 1)
     got3, parts2 = after((got3, parts2), enc_sums)
+    got4 = grid.swap_dp(after(send4, (parts2, got3)), 1)
     held3, sends = core_sum(grid, keep3, got3)
     parts3 = xy_scatter(grid, sends)
     held4, sends = core_sum(grid, keep4, got4)
+    parts3 = after(parts3, sends)
     parts4 = xy_scatter(grid, sends)
 
     def last_swaps(*pieces):

time: 352 us -> 348 us (0.989)
  waiting for transfers between devices: 68.9 us -> 62.3 us
    ppermute x24, waiting for transfers between devices: 44.9 us -> 37.4 us  [swap_dp(): return lax.ppermute(value, 'dp', [(i, i ^ flip) for i in range(self.nd)])]
    unnamed x85 -> x83, local copies, waits for them, and re-layouts: 14 us -> 14.1 us
  transfers between devices with their start and end apart: 38 -> 38, of which waited for: 14 -> 14; matrix products, arithmetic and copies ran while one was open for 7% -> 7% of each run, Pallas kernels for 35% -> 36%
where the time goes in v1:
time: 348 us; the launch traced here: 345 us
  Pallas kernels  191 us (55%)
  waiting for transfers between devices  62.3 us (18%)
  starting transfers between devices  40.3 us (12%)
  local copies, waits for them, and re-layouts  25 us (7%)
  between operations  14.8 us (4%)
  other arithmetic  10.9 us (3%)
    pallas_call x3, Pallas kernels, attend_backward(): pl.pallas_call(functools.partial(attend_backward_kernel, mode, base, piec...  83.1 us
    pallas_call x3, Pallas kernels, attend_forward(): pl.pallas_call(functools.partial(attend_forward_kernel, mode, base, piece...  41.9 us
    ppermute x24, waiting for transfers between devices, swap_dp(): return lax.ppermute(value, 'dp', [(i, i ^ flip) for i in range(self.nd)])  37.4 us
    pallas_call x1, Pallas kernels, feed_both(): pl.pallas_call(functools.partial(feed_both_kernel, base, first, piece, ow...  25.2 us
    ppermute x11, waiting for transfers between devices, swap_fsdp(): return lax.ppermute(value, 'fsdp', [(i, i ^ flip) for i in range(self.nf)])  24.8 us
    ppermute x24, starting transfers between devices, swap_dp(): return lax.ppermute(value, 'dp', [(i, i ^ flip) for i in range(self.nd)])  23.7 us
    pallas_call x1, Pallas kernels, feed_backward(): pl.pallas_call(functools.partial(feed_backward_kernel, base, first, piece...  18.7 us
    ppermute x11, starting transfers between devices, swap_fsdp(): return lax.ppermute(value, 'fsdp', [(i, i ^ flip) for i in range(self.nf)])  16.4 us
  transfers between devices with their start and end apart: 38, of which 14 were waited for; matrix products, arithmetic and copies ran while one was open for 7% of the time, Pallas kernels for 36%

profile of v1, /device:TPU:0, one launch (start us, length us, event | category | flops | bytes accessed | tf_op | source)
XLA Modules:
  0.0 344.6 jit_solution(2079395023522887680)
XLA Ops:
  11.9 5.1 %collective-permute-start.2 = (bf16[144,512]{1,0:T(8,128)(2,1)}, bf16[144,512]{1,0:T(8,128)(2,1)S(1)}, u32[]{:S(2)}, u32[]{:S(2)}) collective-permute-start(bf16[144,512]{1,0:T(8,128)(2,1)} %get-tuple-element.121), channel_id=1, source_target_pairs={{0,3},{1,2},{2,1},{3,0},{4,7},{5,6},{6,5},{7,4},{8,11},{9,10},{10,... | collective-permute-start | bytes 442376 | tf_op jit(solution)/shard_map/ppermute | solution.py:44
  17.7 4.3 %collective-permute-done.2 = bf16[144,512]{1,0:T(8,128)(2,1)S(1)} collective-permute-done((bf16[144,512]{1,0:T(8,128)(2,1)}, bf16[144,512]{1,0:T(8,128)(2,1)S(1)}, u32[]{:S(2)}, u32[]{:S(2)}) %collective-permute-start.2) | collective-permute-done | bytes 147488 | tf_op jit(solution)/shard_map/ppermute | solution.py:44
  22.0 10.0 %collective-permute-done.1 = bf16[144,512]{1,0:T(8,128)(2,1)S(1)} collective-permute-done((bf16[144,512]{1,0:T(8,128)(2,1)}, bf16[144,512]{1,0:T(8,128)(2,1)S(1)}, u32[]{:S(2)}, u32[]{:S(2)}) %collective-permute-start.1) | collective-permute-done | bytes 147488 | tf_op jit(solution)/shard_map/ppermute | solution.py:44
  34.0 3.2 collective-permute-start.5
  37.8 3.4 collective-permute-done.6
  41.4 6.0 %collective-permute-done.5 = bf16[4,80,512]{2,1,0:T(8,128)(2,1)S(1)} collective-permute-done((bf16[4,80,512]{2,1,0:T(8,128)(2,1)S(1)}, bf16[4,80,512]{2,1,0:T(8,128)(2,1)S(1)}, u32[]{:S(2)}, u32[]{:S(2)}) %collective-permute-start.5) | collective-permute-done | bytes 327712 | tf_op jit(solution)/shard_map/ppermute | solution.py:41
  47.4 5.3 %collective-permute-done.4 = bf16[4,80,512]{2,1,0:T(8,128)(2,1)S(1)} collective-permute-done((bf16[4,80,512]{2,1,0:T(8,128)(2,1)S(1)}, bf16[4,80,512]{2,1,0:T(8,128)(2,1)S(1)}, u32[]{:S(2)}, u32[]{:S(2)}) %collective-permute-start.4) | collective-permute-done | bytes 327712 | tf_op jit(solution)/shard_map/ppermute | solution.py:41
  52.7 2.9 collective-permute-done.3
  60.2 14.0 %attend_forward_enc.1 = (bf16[1024,512]{1,0:T(8,128)(2,1)}, bf16[1024,512]{1,0:T(8,128)(2,1)}, bf16[1024,512]{1,0:T(8,128)(2,1)}, f32[1024,512]{1,0:T(8,128)}, b...) custom-call(s32[1]{0:T(128)} %bitcast.refs_0_, ...), custom_call_target="tpu_custom_call" | custom-call | flops 6442450944 | bytes 8388608 | tf_op jit(solution)/shard_map/attend_forward_enc/pallas_call | solution.py:648
  77.9 2.2 collective-permute-start.13
  81.7 13.9 %attend_forward_dec.1 = (bf16[1024,512]{1,0:T(8,128)(2,1)}, bf16[1024,512]{1,0:T(8,128)(2,1)}, bf16[1024,512]{1,0:T(8,128)(2,1)}, f32[1024,512]{1,0:T(8,128)}, b...) custom-call(s32[1]{0:T(128)} %bitcast.refs_0_, ...), custom_call_target="tpu_custom_call" | custom-call | flops 6442450944 | bytes 8388608 | tf_op jit(solution)/shard_map/attend_forward_dec/pallas_call | solution.py:648
  95.6 10.0 %collective-permute-done.15 = bf16[4,128,512]{2,1,0:T(8,128)(2,1)S(1)} collective-permute-done((bf16[4,128,512]{2,1,0:T(8,128)(2,1)S(1)}, bf16[4,128,512]{2,1,0:T(8,128)(2,1)S(1)}, u32[]{:S(2)}, u32[]{:S(2)}) %collective-permute-start.15) | collective-permute-done | bytes 524320 | tf_op jit(solution)/shard_map/ppermute | solution.py:41
  109.5 4.0 %collective-permute-done.16 = bf16[16,128,512]{2,1,0:T(8,128)(2,1)} collective-permute-done((bf16[16,128,512]{2,1,0:T(8,128)(2,1)}, bf16[16,128,512]{2,1,0:T(8,128)(2,1)}, u32[]{:S(2)}, u32[]{:S(2)}) %collective-permute-start.16) | collective-permute-done | bytes 2097184 | tf_op jit(solution)/shard_map/ppermute | solution.py:41
  113.5 14.6 %feed_forward.1 = (bf16[4,1024,512]{2,1,0:T(8,128)(2,1)}, bf16[4,1024,512]{2,1,0:T(8,128)(2,1)}, f32[1024,512]{1,0:T(8,128)}, f32[1024,1]{1,0:T(8,128)}, bf16[1024,512]{1,0:T(8,128)(2,1)S(1)}) custom-call(s32[1]{0:T(128)} %bitcast.refs_0_, bf16[16,8,16,512]{3,2,1,0:T(8,128)(2,1)} %bitcast.13.refs_1_.refs_3_, ...), custom_call_target="tpu_custom_call" | custom-call | flops 4294967296 | bytes 8388608 | tf_op jit(solution)/shard_map/feed_forward/pallas_call | solution.py:717
  128.2 14.0 %attend_forward_cross.1 = (bf16[1024,512]{1,0:T(8,128)(2,1)}, bf16[1024,512]{1,0:T(8,128)(2,1)}, bf16[1024,512]{1,0:T(8,128)(2,1)}, f32[1024,512]{1,0:T(8,128)},...) custom-call(s32[1]{0:T(128)} %bitcast.refs_0_, ...), custom_call_target="tpu_custom_call" | custom-call | flops 6442450944 | bytes 8388608 | tf_op jit(solution)/shard_map/attend_forward_cross/pallas_call | solution.py:648
  142.3 25.2 %feed_both.1 = (bf16[32,12,16,512]{3,2,1,0:T(8,128)(2,1)}, bf16[1024,512]{1,0:T(8,128)(2,1)}, f32[1024,512]{1,0:T(8,128)S(1)}, f32[8,512]{1,0:T(8,128)S(1)}, f32[4,8,512]{2,1,0:T(8,128)S(1)}) custom-call(s32[1]{0:T(128)} %bitcast.refs_0_, bf16[32,12,16,512]{3,2,1,0:T(8,128)(2,1)} %bitcast.193, bf16[32,12,16,512]{3,2,1,0:T(8,128)(2,1)} %bitcast.194, ...), custom_call_target="tpu_custom_call" | custom-call | flops 12884901888 | bytes 8388608 | tf_op jit(solution)/shard_map/feed_both/pallas_call | solution.py:910
  167.5 25.7 %attend_backward_cross.1 = (bf16[32,12,16,512]{3,2,1,0:T(8,128)(2,1)}, f32[1024,512]{1,0:T(8,128)}, f32[8,512]{1,0:T(8,128)S(1)}, f32[1024,512]{1,0:T(8,128)S(1)}) custom-call(s32[1]{0:T(128)} %bitcast.refs_0_, bf16[32,12,16,512]{3,2,1,0:T(8,128)(2,1)} %bitcast.195, bf16[32,12,16,512]{3,2,1,0:T(8,128)(2,1)} %bitcast.196, ...), custom_call_target="tpu_custom_call", output_to_operand_aliasing={{0}: (17, {})} | custom-call | flops 15032385536 | bytes 8388608 | tf_op jit(solution)/shard_map/attend_backward_cross/pallas_call | solution.py:1082
  196.2 18.7 %feed_backward.1 = (bf16[16,8,16,512]{3,2,1,0:T(8,128)(2,1)}, bf16[16,8,16,512]{3,2,1,0:T(8,128)(2,1)}, f32[1024,512]{1,0:T(8,128)}, f32[8,512]{1,0:T(8,128)S(1)}, f32[4,8,512]{2,1,0:T(8,128)S(1)}) custom-call(s32[1]{0:T(128)} %bitcast.refs_0_, bf16[16,8,16,512]{3,2,1,0:T(8,128)(2,1)} %bitcast.13.refs_1_.refs_3_, ...), custom_call_target="tpu_custom_call" | custom-call | flops 8589934592 | bytes 8388608 | tf_op jit(solution)/shard_map/feed_backward/pallas_call | solution.py:801
  215.8 29.1 %attend_backward_dec.1 = (bf16[16,4,16,512]{3,2,1,0:T(8,128)(2,1)}, bf16[16,4,16,512]{3,2,1,0:T(8,128)(2,1)}, bf16[1024,512]{1,0:T(8,128)(2,1)}, f32[8,512]{1,0:T(8,128)S(1)}, f32[128,512]{1,0:T(8,128)S(1)}) custom-call(s32[1]{0:T(128)} %bitcast.refs_0_, bf16[16,4,16,512]{3,2,1,0:T(8,128)(2,1)} %bitcast.179, bf16[16,4,16,512]{3,2,1,0:T(8,128)(2,1)} %bitcast.202, ...), custom_call_target="tpu_custom_call" | custom-call | flops 15032385536 | bytes 8388608 | tf_op jit(solution)/shard_map/attend_backward_dec/pallas_call | solution.py:1082
  249.6 2.0 collective-permute-start.20
  252.0 28.3 %attend_backward_enc.1 = (bf16[16,5,16,512]{3,2,1,0:T(8,128)(2,1)}, bf16[16,5,16,512]{3,2,1,0:T(8,128)(2,1)}, bf16[1024,512]{1,0:T(8,128)(2,1)}, f32[8,512]{1,0:T(8,128)}) custom-call(s32[1]{0:T(128)} %bitcast.refs_0_, bf16[16,5,16,512]{3,2,1,0:T(8,128)(2,1)} %bitcast.162, bf16[16,5,16,512]{3,2,1,0:T(8,128)(2,1)} %bitcast.10.refs_2_.refs_4_.refs_6_, ...), custom_call_target="tpu_custom_call" | custom-call | flops 15032385536 | bytes 8388608 | tf_op jit(solution)/shard_map/attend_backward_enc/pallas_call | solution.py:1082
  285.3 2.0 collective-permute-start.30
  291.8 2.0 collective-permute-start.24
  295.9 4.0 %collective-permute-done.30.refs_8_ = bf16[4,64,512]{2,1,0:T(8,128)(2,1)S(1)} collective-permute-done((bf16[4,64,512]{2,1,0:T(8,128)(2,1)S(1)}, bf16[4,64,512]{2,1,0:T(8,128)(2,1)S(1)}, u32[]{:S(2)}, u32[]{:S(2)}) %collective-permute-start.30) | collective-permute-done | bytes 262176 | tf_op jit(solution)/shard_map/ppermute | solution.py:41
  300.8 3.3 collective-permute-start.32
  308.2 2.3 collective-permute-start.34
  310.6 2.7 collective-permute-done.24.refs_3_
  313.5 2.8 collective-permute-start.28
  321.8 3.5 %collective-permute-done.33.refs_11_ = bf16[192,512]{1,0:T(8,128)(2,1)} collective-permute-done((bf16[192,512]{1,0:T(8,128)(2,1)}, bf16[192,512]{1,0:T(8,128)(2,1)}, u32[]{:S(2)}, u32[]{:S(2)}) %collective-permute-start.33) | collective-permute-done | bytes 196640 | tf_op jit(solution)/shard_map/ppermute | solution.py:44
  326.0 2.3 shards.5
  328.3 3.6 %collective-permute-done.27.refs_6_ = bf16[80,512]{1,0:T(8,128)(2,1)S(1)} collective-permute-done((bf16[80,512]{1,0:T(8,128)(2,1)S(1)}, bf16[80,512]{1,0:T(8,128)(2,1)S(1)}, u32[]{:S(2)}, u32[]{:S(2)}) %collective-permute-start.27) | collective-permute-done | bytes 81952 | tf_op jit(solution)/shard_map/ppermute | solution.py:44
  333.2 2.0 shards.4
  (184 shorter events, 57.4 us)
Async XLA Ops:
  7.2 121.0 %all-gather.3.cloned.1.call-start = ((), (), s32[]{:S(2)}) async-start(), calls=%async_computation.4 | async-start | bytes 6488064 | tf_op jit(solution)/shard_map/all_gather | solution.py:1161
  11.9 270.3 %reduce-scatter.3.cloned.1.call-start = ((), (), s32[]{:S(2)}) async-start(), calls=%async_computation.2 | async-start | bytes 7077888 | tf_op jit(solution)/shard_map/reduce_scatter | solution.py:200
  17.1 14.9 %collective-permute-start.1 = (bf16[144,512]{1,0:T(8,128)(2,1)}, bf16[144,512]{1,0:T(8,128)(2,1)S(1)}, u32[]{:S(2)}, u32[]{:S(2)}) collective-permute-start(bf16[144,512]{1,0:T(8,128)(2,1)} %get-tuple-element.121), channel_id=1, source_target_pairs={{0,2},{1,3},{2,0},{3,1},{4,6},{5,7},{6,4},{7,5},{8,10},{9,11},{10,... | collective-permute-start | bytes 442376 | tf_op jit(solution)/shard_map/ppermute | solution.py:44
  17.1 14.9 %collective-permute-start = (bf16[144,512]{1,0:T(8,128)(2,1)}, bf16[144,512]{1,0:T(8,128)(2,1)S(1)}, u32[]{:S(2)}, u32[]{:S(2)}) collective-permute-start(bf16[144,512]{1,0:T(8,128)(2,1)} %get-tuple-element.121), channel_id=1, source_target_pairs={{0,1},{1,0},{2,3},{3,2},{4,5},{5,4},{6,7},{7,6},{8,9},{9,8},{10,11... | collective-permute-start | bytes 442376 | tf_op jit(solution)/shard_map/ppermute | solution.py:44
  34.0 13.4 %collective-permute-start.5 = (bf16[4,80,512]{2,1,0:T(8,128)(2,1)S(1)}, bf16[4,80,512]{2,1,0:T(8,128)(2,1)S(1)}, u32[]{:S(2)}, u32[]{:S(2)}) collective-permute-start(bf16[4,80,512]{2,1,0:T(8,128)(2,1)S(1)} %slice.383), channel_id=1, source_target_pairs={{0,24},{4,28},{8,16},{12,20},{16,8},{20,12},{24,0},{28,4},{1,25},{... | collective-permute-start | bytes 983048 | tf_op jit(solution)/shard_map/ppermute | solution.py:41
  37.1 15.6 %collective-permute-start.4 = (bf16[4,80,512]{2,1,0:T(8,128)(2,1)S(1)}, bf16[4,80,512]{2,1,0:T(8,128)(2,1)S(1)}, u32[]{:S(2)}, u32[]{:S(2)}) collective-permute-start(bf16[4,80,512]{2,1,0:T(8,128)(2,1)S(1)} %slice.383), channel_id=1, source_target_pairs={{0,16},{4,20},{8,24},{12,28},{16,0},{20,4},{24,8},{28,12},{1,17},{... | collective-permute-start | bytes 983048 | tf_op jit(solution)/shard_map/ppermute | solution.py:41
  37.1 18.5 %collective-permute-start.3 = (bf16[4,80,512]{2,1,0:T(8,128)(2,1)S(1)}, bf16[4,80,512]{2,1,0:T(8,128)(2,1)S(1)}, u32[]{:S(2)}, u32[]{:S(2)}) collective-permute-start(bf16[4,80,512]{2,1,0:T(8,128)(2,1)S(1)} %slice.383), channel_id=1, source_target_pairs={{0,8},{4,12},{8,0},{12,4},{16,24},{20,28},{24,16},{28,20},{1,9},{5... | collective-permute-start | bytes 983048 | tf_op jit(solution)/shard_map/ppermute | solution.py:41
  41.2 14.6 %collective-permute-start.7 = (bf16[2,128,512]{2,1,0:T(8,128)(2,1)S(1)}, bf16[2,128,512]{2,1,0:T(8,128)(2,1)S(1)}, u32[]{:S(2)}, u32[]{:S(2)}) collective-permute-start(bf16[2,128,512]{2,1,0:T(8,128)(2,1)S(1)} %pad_maximum_fusion.4), channel_id=1, source_target_pairs={{0,1},{1,0},{2,3},{3,2},{4,5},{5,4},{6,7},{7,6},{8,9},{9,8},{10,11... | collective-permute-start | bytes 786440 | tf_op jit(solution)/shard_map/ppermute | solution.py:44
  56.6 17.6 %collective-permute-start.11 = (bf16[4,64,512]{2,1,0:T(8,128)(2,1)S(1)}, bf16[4,64,512]{2,1,0:T(8,128)(2,1)S(1)}, u32[]{:S(2)}, u32[]{:S(2)}) collective-permute-start(bf16[4,64,512]{2,1,0:T(8,128)(2,1)S(1)} %pad_maximum_fusion.3), channel_id=1, source_target_pairs={{0,24},{4,28},{8,16},{12,20},{16,8},{20,12},{24,0},{28,4},{1,25},{... | collective-permute-start | bytes 786440 | tf_op jit(solution)/shard_map/ppermute | solution.py:41
  58.1 18.0 %collective-permute-start.10 = (bf16[4,64,512]{2,1,0:T(8,128)(2,1)S(1)}, bf16[4,64,512]{2,1,0:T(8,128)(2,1)S(1)}, u32[]{:S(2)}, u32[]{:S(2)}) collective-permute-start(bf16[4,64,512]{2,1,0:T(8,128)(2,1)S(1)} %pad_maximum_fusion.3), channel_id=1, source_target_pairs={{0,16},{4,20},{8,24},{12,28},{16,0},{20,4},{24,8},{28,12},{1,17},{... | collective-permute-start | bytes 786440 | tf_op jit(solution)/shard_map/ppermute | solution.py:41
  59.8 16.4 %collective-permute-start.9 = (bf16[4,64,512]{2,1,0:T(8,128)(2,1)S(1)}, bf16[4,64,512]{2,1,0:T(8,128)(2,1)S(1)}, u32[]{:S(2)}, u32[]{:S(2)}) collective-permute-start(bf16[4,64,512]{2,1,0:T(8,128)(2,1)S(1)} %pad_maximum_fusion.3), channel_id=1, source_target_pairs={{0,8},{4,12},{8,0},{12,4},{16,24},{20,28},{24,16},{28,20},{1,9},{5... | collective-permute-start | bytes 786440 | tf_op jit(solution)/shard_map/ppermute | solution.py:41
  77.2 18.4 %collective-permute-start.14 = (bf16[4,128,512]{2,1,0:T(8,128)(2,1)S(1)}, bf16[4,128,512]{2,1,0:T(8,128)(2,1)S(1)}, u32[]{:S(2)}, u32[]{:S(2)}) collective-permute-start(bf16[4,128,512]{2,1,0:T(8,128)(2,1)S(1)} %pad_maximum_fusion.2), channel_id=1, source_target_pairs={{0,16},{4,20},{8,24},{12,28},{16,0},{20,4},{24,8},{28,12},{1,17},{... | collective-permute-start | bytes 1572872 | tf_op jit(solution)/shard_map/ppermute | solution.py:41
  77.9 17.7 %collective-permute-start.13 = (bf16[4,128,512]{2,1,0:T(8,128)(2,1)S(1)}, bf16[4,128,512]{2,1,0:T(8,128)(2,1)S(1)}, u32[]{:S(2)}, u32[]{:S(2)}) collective-permute-start(bf16[4,128,512]{2,1,0:T(8,128)(2,1)S(1)} %pad_maximum_fusion.2), channel_id=1, source_target_pairs={{0,8},{4,12},{8,0},{12,4},{16,24},{20,28},{24,16},{28,20},{1,9},{5... | collective-permute-start | bytes 1572872 | tf_op jit(solution)/shard_map/ppermute | solution.py:41
  80.1 25.6 %collective-permute-start.15 = (bf16[4,128,512]{2,1,0:T(8,128)(2,1)S(1)}, bf16[4,128,512]{2,1,0:T(8,128)(2,1)S(1)}, u32[]{:S(2)}, u32[]{:S(2)}) collective-permute-start(bf16[4,128,512]{2,1,0:T(8,128)(2,1)S(1)} %pad_maximum_fusion.2), channel_id=1, source_target_pairs={{0,24},{4,28},{8,16},{12,20},{16,8},{20,12},{24,0},{28,4},{1,25},{... | collective-permute-start | bytes 1572872 | tf_op jit(solution)/shard_map/ppermute | solution.py:41
  194.6 112.0 %reduce-scatter.5.cloned.1.call-start = ((), (), s32[]{:S(2)}) async-start(), calls=%async_computation.3 | async-start | bytes 983040 | tf_op jit(solution)/shard_map/reduce_scatter | solution.py:203
  214.9 31.7 %collective-permute-start.17 = (bf16[16,128,512]{2,1,0:T(8,128)(2,1)}, bf16[16,128,512]{2,1,0:T(8,128)(2,1)}, u32[]{:S(2)}, u32[]{:S(2)}) collective-permute-start(bf16[16,128,512]{2,1,0:T(8,128)(2,1)} %bitcast.198), channel_id=1, source_target_pairs={{0,4},{4,0},{8,12},{12,8},{16,20},{20,16},{24,28},{28,24},{1,5},{5... | collective-permute-start | bytes 6291464 | tf_op jit(solution)/shard_map/ppermute | solution.py:41
  244.9 35.4 %collective-permute-start.18 = (bf16[16,64,512]{2,1,0:T(8,128)(2,1)}, bf16[16,64,512]{2,1,0:T(8,128)(2,1)S(1)}, u32[]{:S(2)}, u32[]{:S(2)}) collective-permute-start(bf16[16,64,512]{2,1,0:T(8,128)(2,1)} %bitcast.204), channel_id=1, source_target_pairs={{0,4},{4,0},{8,12},{12,8},{16,20},{20,16},{24,28},{28,24},{1,5},{5... | collective-permute-start | bytes 3145736 | tf_op jit(solution)/shard_map/ppermute | solution.py:41
  248.4 31.9 %collective-permute-start.21 = (bf16[4,128,512]{2,1,0:T(8,128)(2,1)S(1)}, bf16[4,128,512]{2,1,0:T(8,128)(2,1)S(1)}, u32[]{:S(2)}, u32[]{:S(2)}) collective-permute-start(bf16[4,128,512]{2,1,0:T(8,128)(2,1)S(1)} %get-tuple-element.315), channel_id=1, source_target_pairs={{0,24},{4,28},{8,16},{12,20},{16,8},{20,12},{24,0},{28,4},{1,25},{... | collective-permute-start | bytes 1572872 | tf_op jit(solution)/shard_map/ppermute | solution.py:41
  249.6 30.7 %collective-permute-start.20 = (bf16[4,128,512]{2,1,0:T(8,128)(2,1)S(1)}, bf16[4,128,512]{2,1,0:T(8,128)(2,1)S(1)}, u32[]{:S(2)}, u32[]{:S(2)}) collective-permute-start(bf16[4,128,512]{2,1,0:T(8,128)(2,1)S(1)} %get-tuple-element.316), channel_id=1, source_target_pairs={{0,16},{4,20},{8,24},{12,28},{16,0},{20,4},{24,8},{28,12},{1,17},{... | collective-permute-start | bytes 1572872 | tf_op jit(solution)/shard_map/ppermute | solution.py:41
  251.7 28.7 %collective-permute-start.19 = (bf16[4,128,512]{2,1,0:T(8,128)(2,1)S(1)}, bf16[4,128,512]{2,1,0:T(8,128)(2,1)S(1)}, u32[]{:S(2)}, u32[]{:S(2)}) collective-permute-start(bf16[4,128,512]{2,1,0:T(8,128)(2,1)S(1)} %get-tuple-element.317), channel_id=1, source_target_pairs={{0,8},{4,12},{8,0},{12,4},{16,24},{20,28},{24,16},{28,20},{1,9},{5... | collective-permute-start | bytes 1572872 | tf_op jit(solution)/shard_map/ppermute | solution.py:41
  284.1 10.1 %collective-permute-start.31 = (bf16[4,64,512]{2,1,0:T(8,128)(2,1)S(1)}, bf16[4,64,512]{2,1,0:T(8,128)(2,1)S(1)}, u32[]{:S(2)}, u32[]{:S(2)}) collective-permute-start(bf16[4,64,512]{2,1,0:T(8,128)(2,1)S(1)} %get-tuple-element.334), channel_id=1, source_target_pairs={{0,24},{4,28},{8,16},{12,20},{16,8},{20,12},{24,0},{28,4},{1,25},{... | collective-permute-start | bytes 786440 | tf_op jit(solution)/shard_map/ppermute | solution.py:41
  285.3 14.6 %collective-permute-start.30 = (bf16[4,64,512]{2,1,0:T(8,128)(2,1)S(1)}, bf16[4,64,512]{2,1,0:T(8,128)(2,1)S(1)}, u32[]{:S(2)}, u32[]{:S(2)}) collective-permute-start(bf16[4,64,512]{2,1,0:T(8,128)(2,1)S(1)} %get-tuple-element.335), channel_id=1, source_target_pairs={{0,16},{4,20},{8,24},{12,28},{16,0},{20,4},{24,8},{28,12},{1,17},{... | collective-permute-start | bytes 786440 | tf_op jit(solution)/shard_map/ppermute | solution.py:41
  287.3 12.6 %collective-permute-start.29 = (bf16[4,64,512]{2,1,0:T(8,128)(2,1)S(1)}, bf16[4,64,512]{2,1,0:T(8,128)(2,1)S(1)}, u32[]{:S(2)}, u32[]{:S(2)}) collective-permute-start(bf16[4,64,512]{2,1,0:T(8,128)(2,1)S(1)} %get-tuple-element.336), channel_id=1, source_target_pairs={{0,8},{4,12},{8,0},{12,4},{16,24},{20,28},{24,16},{28,20},{1,9},{5... | collective-permute-start | bytes 786440 | tf_op jit(solution)/shard_map/ppermute | solution.py:41
  290.6 17.7 %collective-permute-start.25 = (bf16[4,80,512]{2,1,0:T(8,128)(2,1)S(1)}, bf16[4,80,512]{2,1,0:T(8,128)(2,1)S(1)}, u32[]{:S(2)}, u32[]{:S(2)}) collective-permute-start(bf16[4,80,512]{2,1,0:T(8,128)(2,1)S(1)} %get-tuple-element.324), channel_id=1, source_target_pairs={{0,24},{4,28},{8,16},{12,20},{16,8},{20,12},{24,0},{28,4},{1,25},{... | collective-permute-start | bytes 983048 | tf_op jit(solution)/shard_map/ppermute | solution.py:41
  291.8 21.5 %collective-permute-start.24 = (bf16[4,80,512]{2,1,0:T(8,128)(2,1)S(1)}, bf16[4,80,512]{2,1,0:T(8,128)(2,1)S(1)}, u32[]{:S(2)}, u32[]{:S(2)}) collective-permute-start(bf16[4,80,512]{2,1,0:T(8,128)(2,1)S(1)} %get-tuple-element.325), channel_id=1, source_target_pairs={{0,16},{4,20},{8,24},{12,28},{16,0},{20,4},{24,8},{28,12},{1,17},{... | collective-permute-start | bytes 983048 | tf_op jit(solution)/shard_map/ppermute | solution.py:41
  294.2 19.0 %collective-permute-start.23 = (bf16[4,80,512]{2,1,0:T(8,128)(2,1)S(1)}, bf16[4,80,512]{2,1,0:T(8,128)(2,1)S(1)}, u32[]{:S(2)}, u32[]{:S(2)}) collective-permute-start(bf16[4,80,512]{2,1,0:T(8,128)(2,1)S(1)} %get-tuple-element.326), channel_id=1, source_target_pairs={{0,8},{4,12},{8,0},{12,4},{16,24},{20,28},{24,16},{28,20},{1,9},{5... | collective-permute-start | bytes 983048 | tf_op jit(solution)/shard_map/ppermute | solution.py:41
  300.8 17.5 %collective-permute-start.32 = (bf16[192,512]{1,0:T(8,128)(2,1)}, bf16[192,512]{1,0:T(8,128)(2,1)}, u32[]{:S(2)}, u32[]{:S(2)}) collective-permute-start(bf16[192,512]{1,0:T(8,128)(2,1)} %pad_maximum_fusion.5), channel_id=1, source_target_pairs={{0,1},{1,0},{2,3},{3,2},{4,5},{5,4},{6,7},{7,6},{8,9},{9,8},{10,11... | collective-permute-start | bytes 589832 | tf_op jit(solution)/shard_map/ppermute | solution.py:44
  304.7 20.5 %collective-permute-start.33 = (bf16[192,512]{1,0:T(8,128)(2,1)}, bf16[192,512]{1,0:T(8,128)(2,1)}, u32[]{:S(2)}, u32[]{:S(2)}) collective-permute-start(bf16[192,512]{1,0:T(8,128)(2,1)} %pad_maximum_fusion.6), channel_id=1, source_target_pairs={{0,2},{1,3},{2,0},{3,1},{4,6},{5,7},{6,4},{7,5},{8,10},{9,11},{10,... | collective-permute-start | bytes 589832 | tf_op jit(solution)/shard_map/ppermute | solution.py:44
  308.2 17.1 %collective-permute-start.34 = (bf16[192,512]{1,0:T(8,128)(2,1)}, bf16[192,512]{1,0:T(8,128)(2,1)S(1)}, u32[]{:S(2)}, u32[]{:S(2)}) collective-permute-start(bf16[192,512]{1,0:T(8,128)(2,1)} %pad_maximum_fusion.7), channel_id=1, source_target_pairs={{0,3},{1,2},{2,1},{3,0},{4,7},{5,6},{6,5},{7,4},{8,11},{9,10},{10,... | collective-permute-start | bytes 589832 | tf_op jit(solution)/shard_map/ppermute | solution.py:44
  313.5 14.8 %collective-permute-start.28 = (bf16[80,512]{1,0:T(8,128)(2,1)S(1)}, bf16[80,512]{1,0:T(8,128)(2,1)S(1)}, u32[]{:S(2)}, u32[]{:S(2)}) collective-permute-start(bf16[80,512]{1,0:T(8,128)(2,1)S(1)} %get-tuple-element.321), channel_id=1, source_target_pairs={{0,3},{1,2},{2,1},{3,0},{4,7},{5,6},{6,5},{7,4},{8,11},{9,10},{10,... | collective-permute-start | bytes 245768 | tf_op jit(solution)/shard_map/ppermute | solution.py:44
  316.3 15.6 %collective-permute-start.27 = (bf16[80,512]{1,0:T(8,128)(2,1)S(1)}, bf16[80,512]{1,0:T(8,128)(2,1)S(1)}, u32[]{:S(2)}, u32[]{:S(2)}) collective-permute-start(bf16[80,512]{1,0:T(8,128)(2,1)S(1)} %get-tuple-element.322), channel_id=1, source_target_pairs={{0,2},{1,3},{2,0},{3,1},{4,6},{5,7},{6,4},{7,5},{8,10},{9,11},{10,... | collective-permute-start | bytes 245768 | tf_op jit(solution)/shard_map/ppermute | solution.py:44
  318.2 13.7 %collective-permute-start.26 = (bf16[80,512]{1,0:T(8,128)(2,1)S(1)}, bf16[80,512]{1,0:T(8,128)(2,1)S(1)}, u32[]{:S(2)}, u32[]{:S(2)}) collective-permute-start(bf16[80,512]{1,0:T(8,128)(2,1)S(1)} %get-tuple-element.323), channel_id=1, source_target_pairs={{0,1},{1,0},{2,3},{3,2},{4,5},{5,4},{6,7},{7,6},{8,9},{9,8},{10,11... | collective-permute-start | bytes 245768 | tf_op jit(solution)/shard_map/ppermute | solution.py:44
  (41 other events, 459.6 us)
Sparse Core Ops, SparseCore 0:
  12.0 84.6 all-gather.2
  194.7 75.8 reduce-scatter.2
  282.3 23.2 reduce-scatter.4

commit v2 on v1

--- a/solution.py
+++ b/solution.py
@@ -794,7 +794,7 @@
 def feed_backward(base, first, me, piece, own, grads, at, vectors, grad, n2, inv2, n1, act, slope):
     tokens = n1.shape[0]
     weights = list(piece.arrays[own]) + list(piece.arrays[own + 1])
-    act, slope, n2, inv2, n1 = (near_not(a) for a in (act, slope, n2, inv2, n1))
+    act, slope, n2, inv2, n1, grad = (near_not(a) for a in (act, slope, n2, inv2, n1, grad))
     held = [vectors, grad, n2, inv2, n1]
     chunk_spec = pl.BlockSpec((1, tokens, 512), lambda i: (i, 0, 0))
     outs = [like(tokens, 512, F32), like(8, 512, F32), jax.ShapeDtypeStruct((4, 8, 512), F32)]
@@ -1063,8 +1063,8 @@
     outs = [like(tokens, 512, F32 if mode == "cross" else BF), like(8, 512, F32)]
     out_specs = [row_spec(outs[0]), whole_spec(outs[1])]
     if mode == "cross":
-        outs.append(like(tokens, 512, F32))
-        out_specs.append(row_spec(outs[-1]))
+        outs.append(far(like(tokens, 512, F32)))
+        out_specs.append(row_spec(like(tokens, 512, F32)))
     if mode == "dec":
         outs.append(like(128, 512, F32))
         out_specs.append(whole_spec(outs[-1]))

time: 348 us -> 346 us (level)
    unnamed x83 -> x79, local copies, waits for them, and re-layouts: 14.1 us -> 11.1 us
where the time goes in v2:
time: 346 us; the launch traced here: 342 us
  Pallas kernels  192 us (55%)
  waiting for transfers between devices  63.1 us (18%)
  starting transfers between devices  39.1 us (11%)
  local copies, waits for them, and re-layouts  22.1 us (6%)
  between operations  14.8 us (4%)
  other arithmetic  10.9 us (3%)
    pallas_call x3, Pallas kernels, attend_backward(): pl.pallas_call(functools.partial(attend_backward_kernel, mode, base, piec...  83.6 us
    pallas_call x3, Pallas kernels, attend_forward(): pl.pallas_call(functools.partial(attend_forward_kernel, mode, base, piece...  41.9 us
    ppermute x24, waiting for transfers between devices, swap_dp(): return lax.ppermute(value, 'dp', [(i, i ^ flip) for i in range(self.nd)])  38.2 us
    pallas_call x1, Pallas kernels, feed_both(): pl.pallas_call(functools.partial(feed_both_kernel, base, first, piece, ow...  25.1 us
    ppermute x11, waiting for transfers between devices, swap_fsdp(): return lax.ppermute(value, 'fsdp', [(i, i ^ flip) for i in range(self.nf)])  24.8 us
    ppermute x24, starting transfers between devices, swap_dp(): return lax.ppermute(value, 'dp', [(i, i ^ flip) for i in range(self.nd)])  23.2 us
    pallas_call x1, Pallas kernels, feed_backward(): pl.pallas_call(functools.partial(feed_backward_kernel, base, first, piece...  19.1 us
    ppermute x11, starting transfers between devices, swap_fsdp(): return lax.ppermute(value, 'fsdp', [(i, i ^ flip) for i in range(self.nf)])  15.8 us
  transfers between devices with their start and end apart: 38, of which 14 were waited for; matrix products, arithmetic and copies ran while one was open for 7% of the time, Pallas kernels for 36%

profile of v2, /device:TPU:0, one launch (start us, length us, event | category | flops | bytes accessed | tf_op | source)
XLA Modules:
  0.0 342.3 jit_solution(14258484711050635384)
XLA Ops:
  11.9 5.1 %collective-permute-start.2 = (bf16[144,512]{1,0:T(8,128)(2,1)}, bf16[144,512]{1,0:T(8,128)(2,1)S(1)}, u32[]{:S(2)}, u32[]{:S(2)}) collective-permute-start(bf16[144,512]{1,0:T(8,128)(2,1)} %get-tuple-element.121), channel_id=1, source_target_pairs={{0,3},{1,2},{2,1},{3,0},{4,7},{5,6},{6,5},{7,4},{8,11},{9,10},{10,... | collective-permute-start | bytes 442376 | tf_op jit(solution)/shard_map/ppermute | solution.py:44
  17.7 4.3 %collective-permute-done.2 = bf16[144,512]{1,0:T(8,128)(2,1)S(1)} collective-permute-done((bf16[144,512]{1,0:T(8,128)(2,1)}, bf16[144,512]{1,0:T(8,128)(2,1)S(1)}, u32[]{:S(2)}, u32[]{:S(2)}) %collective-permute-start.2) | collective-permute-done | bytes 147488 | tf_op jit(solution)/shard_map/ppermute | solution.py:44
  22.0 10.0 %collective-permute-done.1 = bf16[144,512]{1,0:T(8,128)(2,1)S(1)} collective-permute-done((bf16[144,512]{1,0:T(8,128)(2,1)}, bf16[144,512]{1,0:T(8,128)(2,1)S(1)}, u32[]{:S(2)}, u32[]{:S(2)}) %collective-permute-start.1) | collective-permute-done | bytes 147488 | tf_op jit(solution)/shard_map/ppermute | solution.py:44
  34.0 3.2 collective-permute-start.5
  37.8 3.4 collective-permute-done.6
  41.4 6.0 %collective-permute-done.5 = bf16[4,80,512]{2,1,0:T(8,128)(2,1)S(1)} collective-permute-done((bf16[4,80,512]{2,1,0:T(8,128)(2,1)S(1)}, bf16[4,80,512]{2,1,0:T(8,128)(2,1)S(1)}, u32[]{:S(2)}, u32[]{:S(2)}) %collective-permute-start.5) | collective-permute-done | bytes 327712 | tf_op jit(solution)/shard_map/ppermute | solution.py:41
  47.4 5.3 %collective-permute-done.4 = bf16[4,80,512]{2,1,0:T(8,128)(2,1)S(1)} collective-permute-done((bf16[4,80,512]{2,1,0:T(8,128)(2,1)S(1)}, bf16[4,80,512]{2,1,0:T(8,128)(2,1)S(1)}, u32[]{:S(2)}, u32[]{:S(2)}) %collective-permute-start.4) | collective-permute-done | bytes 327712 | tf_op jit(solution)/shard_map/ppermute | solution.py:41
  52.7 2.9 collective-permute-done.3
  60.2 14.0 %attend_forward_enc.1 = (bf16[1024,512]{1,0:T(8,128)(2,1)}, bf16[1024,512]{1,0:T(8,128)(2,1)}, bf16[1024,512]{1,0:T(8,128)(2,1)}, f32[1024,512]{1,0:T(8,128)}, b...) custom-call(s32[1]{0:T(128)} %bitcast.refs_0_, ...), custom_call_target="tpu_custom_call" | custom-call | flops 6442450944 | bytes 8388608 | tf_op jit(solution)/shard_map/attend_forward_enc/pallas_call | solution.py:648
  77.9 2.2 collective-permute-start.13
  81.7 13.8 %attend_forward_dec.1 = (bf16[1024,512]{1,0:T(8,128)(2,1)}, bf16[1024,512]{1,0:T(8,128)(2,1)}, bf16[1024,512]{1,0:T(8,128)(2,1)}, f32[1024,512]{1,0:T(8,128)}, b...) custom-call(s32[1]{0:T(128)} %bitcast.refs_0_, ...), custom_call_target="tpu_custom_call" | custom-call | flops 6442450944 | bytes 8388608 | tf_op jit(solution)/shard_map/attend_forward_dec/pallas_call | solution.py:648
  95.6 10.0 %collective-permute-done.15 = bf16[4,128,512]{2,1,0:T(8,128)(2,1)S(1)} collective-permute-done((bf16[4,128,512]{2,1,0:T(8,128)(2,1)S(1)}, bf16[4,128,512]{2,1,0:T(8,128)(2,1)S(1)}, u32[]{:S(2)}, u32[]{:S(2)}) %collective-permute-start.15) | collective-permute-done | bytes 524320 | tf_op jit(solution)/shard_map/ppermute | solution.py:41
  109.5 4.0 %collective-permute-done.16 = bf16[16,128,512]{2,1,0:T(8,128)(2,1)} collective-permute-done((bf16[16,128,512]{2,1,0:T(8,128)(2,1)}, bf16[16,128,512]{2,1,0:T(8,128)(2,1)}, u32[]{:S(2)}, u32[]{:S(2)}) %collective-permute-start.16) | collective-permute-done | bytes 2097184 | tf_op jit(solution)/shard_map/ppermute | solution.py:41
  113.5 14.6 %feed_forward.1 = (bf16[4,1024,512]{2,1,0:T(8,128)(2,1)}, bf16[4,1024,512]{2,1,0:T(8,128)(2,1)}, f32[1024,512]{1,0:T(8,128)}, f32[1024,1]{1,0:T(8,128)}, bf16[1024,512]{1,0:T(8,128)(2,1)S(1)}) custom-call(s32[1]{0:T(128)} %bitcast.refs_0_, bf16[16,8,16,512]{3,2,1,0:T(8,128)(2,1)} %bitcast.13.refs_1_.refs_3_, ...), custom_call_target="tpu_custom_call" | custom-call | flops 4294967296 | bytes 8388608 | tf_op jit(solution)/shard_map/feed_forward/pallas_call | solution.py:717
  128.2 14.0 %attend_forward_cross.1 = (bf16[1024,512]{1,0:T(8,128)(2,1)}, bf16[1024,512]{1,0:T(8,128)(2,1)}, bf16[1024,512]{1,0:T(8,128)(2,1)}, f32[1024,512]{1,0:T(8,128)},...) custom-call(s32[1]{0:T(128)} %bitcast.refs_0_, ...), custom_call_target="tpu_custom_call" | custom-call | flops 6442450944 | bytes 8388608 | tf_op jit(solution)/shard_map/attend_forward_cross/pallas_call | solution.py:648
  142.2 25.1 %feed_both.1 = (bf16[32,12,16,512]{3,2,1,0:T(8,128)(2,1)}, bf16[1024,512]{1,0:T(8,128)(2,1)}, f32[1024,512]{1,0:T(8,128)S(1)}, f32[8,512]{1,0:T(8,128)S(1)}, f32[4,8,512]{2,1,0:T(8,128)S(1)}) custom-call(s32[1]{0:T(128)} %bitcast.refs_0_, bf16[32,12,16,512]{3,2,1,0:T(8,128)(2,1)} %bitcast.193, bf16[32,12,16,512]{3,2,1,0:T(8,128)(2,1)} %bitcast.194, ...), custom_call_target="tpu_custom_call" | custom-call | flops 12884901888 | bytes 8388608 | tf_op jit(solution)/shard_map/feed_both/pallas_call | solution.py:910
  167.4 26.1 %attend_backward_cross.1 = (bf16[32,12,16,512]{3,2,1,0:T(8,128)(2,1)}, f32[1024,512]{1,0:T(8,128)}, f32[8,512]{1,0:T(8,128)S(1)}, f32[1024,512]{1,0:T(8,128)}) custom-call(s32[1]{0:T(128)} %bitcast.refs_0_, bf16[32,12,16,512]{3,2,1,0:T(8,128)(2,1)} %bitcast.195, bf16[32,12,16,512]{3,2,1,0:T(8,128)(2,1)} %bitcast.196, ...), custom_call_target="tpu_custom_call", output_to_operand_aliasing={{0}: (17, {})} | custom-call | flops 15032385536 | bytes 8388608 | tf_op jit(solution)/shard_map/attend_backward_cross/pallas_call | solution.py:1082
  193.5 19.1 %feed_backward.1 = (bf16[16,8,16,512]{3,2,1,0:T(8,128)(2,1)}, bf16[16,8,16,512]{3,2,1,0:T(8,128)(2,1)}, f32[1024,512]{1,0:T(8,128)}, f32[8,512]{1,0:T(8,128)S(1)}, f32[4,8,512]{2,1,0:T(8,128)S(1)}) custom-call(s32[1]{0:T(128)} %bitcast.refs_0_, bf16[16,8,16,512]{3,2,1,0:T(8,128)(2,1)} %bitcast.13.refs_1_.refs_3_, ...), custom_call_target="tpu_custom_call" | custom-call | flops 8589934592 | bytes 8388608 | tf_op jit(solution)/shard_map/feed_backward/pallas_call | solution.py:801
  213.4 29.2 %attend_backward_dec.1 = (bf16[16,4,16,512]{3,2,1,0:T(8,128)(2,1)}, bf16[16,4,16,512]{3,2,1,0:T(8,128)(2,1)}, bf16[1024,512]{1,0:T(8,128)(2,1)}, f32[8,512]{1,0:T(8,128)S(1)}, f32[128,512]{1,0:T(8,128)S(1)}) custom-call(s32[1]{0:T(128)} %bitcast.refs_0_, bf16[16,4,16,512]{3,2,1,0:T(8,128)(2,1)} %bitcast.179, bf16[16,4,16,512]{3,2,1,0:T(8,128)(2,1)} %bitcast.202, ...), custom_call_target="tpu_custom_call" | custom-call | flops 15032385536 | bytes 8388608 | tf_op jit(solution)/shard_map/attend_backward_dec/pallas_call | solution.py:1082
  246.4 2.8 collective-permute-start.20
  249.9 28.4 %attend_backward_enc.1 = (bf16[16,5,16,512]{3,2,1,0:T(8,128)(2,1)}, bf16[16,5,16,512]{3,2,1,0:T(8,128)(2,1)}, bf16[1024,512]{1,0:T(8,128)(2,1)}, f32[8,512]{1,0:T(8,128)}) custom-call(s32[1]{0:T(128)} %bitcast.refs_0_, bf16[16,5,16,512]{3,2,1,0:T(8,128)(2,1)} %bitcast.162, bf16[16,5,16,512]{3,2,1,0:T(8,128)(2,1)} %bitcast.10.refs_2_.refs_4_.refs_6_, ...), custom_call_target="tpu_custom_call" | custom-call | flops 15032385536 | bytes 8388608 | tf_op jit(solution)/shard_map/attend_backward_enc/pallas_call | solution.py:1082
  283.0 2.0 collective-permute-start.30
  289.4 2.0 collective-permute-start.24
  293.7 4.2 %collective-permute-done.30.refs_8_ = bf16[4,64,512]{2,1,0:T(8,128)(2,1)S(1)} collective-permute-done((bf16[4,64,512]{2,1,0:T(8,128)(2,1)S(1)}, bf16[4,64,512]{2,1,0:T(8,128)(2,1)S(1)}, u32[]{:S(2)}, u32[]{:S(2)}) %collective-permute-start.30) | collective-permute-done | bytes 262176 | tf_op jit(solution)/shard_map/ppermute | solution.py:41
  298.7 2.9 collective-permute-start.32
  305.8 2.4 collective-permute-start.34
  308.2 3.0 collective-permute-done.24.refs_3_
  311.4 2.1 collective-permute-start.28
  313.5 2.4 collective-permute-start.27
  319.4 3.8 %collective-permute-done.33.refs_11_ = bf16[192,512]{1,0:T(8,128)(2,1)} collective-permute-done((bf16[192,512]{1,0:T(8,128)(2,1)}, bf16[192,512]{1,0:T(8,128)(2,1)}, u32[]{:S(2)}, u32[]{:S(2)}) %collective-permute-start.33) | collective-permute-done | bytes 196640 | tf_op jit(solution)/shard_map/ppermute | solution.py:44
  323.8 2.3 shards.5
  326.2 3.4 collective-permute-done.27.refs_6_
  (180 shorter events, 53.3 us)
Async XLA Ops:
  7.2 121.0 %all-gather.3.cloned.1.call-start = ((), (), s32[]{:S(2)}) async-start(), calls=%async_computation.4 | async-start | bytes 6488064 | tf_op jit(solution)/shard_map/all_gather | solution.py:1161
  11.9 268.3 %reduce-scatter.3.cloned.1.call-start = ((), (), s32[]{:S(2)}) async-start(), calls=%async_computation.2 | async-start | bytes 7077888 | tf_op jit(solution)/shard_map/reduce_scatter | solution.py:200
  17.1 14.9 %collective-permute-start.1 = (bf16[144,512]{1,0:T(8,128)(2,1)}, bf16[144,512]{1,0:T(8,128)(2,1)S(1)}, u32[]{:S(2)}, u32[]{:S(2)}) collective-permute-start(bf16[144,512]{1,0:T(8,128)(2,1)} %get-tuple-element.121), channel_id=1, source_target_pairs={{0,2},{1,3},{2,0},{3,1},{4,6},{5,7},{6,4},{7,5},{8,10},{9,11},{10,... | collective-permute-start | bytes 442376 | tf_op jit(solution)/shard_map/ppermute | solution.py:44
  17.1 14.9 %collective-permute-start = (bf16[144,512]{1,0:T(8,128)(2,1)}, bf16[144,512]{1,0:T(8,128)(2,1)S(1)}, u32[]{:S(2)}, u32[]{:S(2)}) collective-permute-start(bf16[144,512]{1,0:T(8,128)(2,1)} %get-tuple-element.121), channel_id=1, source_target_pairs={{0,1},{1,0},{2,3},{3,2},{4,5},{5,4},{6,7},{7,6},{8,9},{9,8},{10,11... | collective-permute-start | bytes 442376 | tf_op jit(solution)/shard_map/ppermute | solution.py:44
  34.0 13.4 %collective-permute-start.5 = (bf16[4,80,512]{2,1,0:T(8,128)(2,1)S(1)}, bf16[4,80,512]{2,1,0:T(8,128)(2,1)S(1)}, u32[]{:S(2)}, u32[]{:S(2)}) collective-permute-start(bf16[4,80,512]{2,1,0:T(8,128)(2,1)S(1)} %slice.383), channel_id=1, source_target_pairs={{0,24},{4,28},{8,16},{12,20},{16,8},{20,12},{24,0},{28,4},{1,25},{... | collective-permute-start | bytes 983048 | tf_op jit(solution)/shard_map/ppermute | solution.py:41
  37.1 15.6 %collective-permute-start.4 = (bf16[4,80,512]{2,1,0:T(8,128)(2,1)S(1)}, bf16[4,80,512]{2,1,0:T(8,128)(2,1)S(1)}, u32[]{:S(2)}, u32[]{:S(2)}) collective-permute-start(bf16[4,80,512]{2,1,0:T(8,128)(2,1)S(1)} %slice.383), channel_id=1, source_target_pairs={{0,16},{4,20},{8,24},{12,28},{16,0},{20,4},{24,8},{28,12},{1,17},{... | collective-permute-start | bytes 983048 | tf_op jit(solution)/shard_map/ppermute | solution.py:41
  37.1 18.5 %collective-permute-start.3 = (bf16[4,80,512]{2,1,0:T(8,128)(2,1)S(1)}, bf16[4,80,512]{2,1,0:T(8,128)(2,1)S(1)}, u32[]{:S(2)}, u32[]{:S(2)}) collective-permute-start(bf16[4,80,512]{2,1,0:T(8,128)(2,1)S(1)} %slice.383), channel_id=1, source_target_pairs={{0,8},{4,12},{8,0},{12,4},{16,24},{20,28},{24,16},{28,20},{1,9},{5... | collective-permute-start | bytes 983048 | tf_op jit(solution)/shard_map/ppermute | solution.py:41
  41.2 14.6 %collective-permute-start.7 = (bf16[2,128,512]{2,1,0:T(8,128)(2,1)S(1)}, bf16[2,128,512]{2,1,0:T(8,128)(2,1)S(1)}, u32[]{:S(2)}, u32[]{:S(2)}) collective-permute-start(bf16[2,128,512]{2,1,0:T(8,128)(2,1)S(1)} %pad_maximum_fusion.4), channel_id=1, source_target_pairs={{0,1},{1,0},{2,3},{3,2},{4,5},{5,4},{6,7},{7,6},{8,9},{9,8},{10,11... | collective-permute-start | bytes 786440 | tf_op jit(solution)/shard_map/ppermute | solution.py:44
  56.6 17.6 %collective-permute-start.11 = (bf16[4,64,512]{2,1,0:T(8,128)(2,1)S(1)}, bf16[4,64,512]{2,1,0:T(8,128)(2,1)S(1)}, u32[]{:S(2)}, u32[]{:S(2)}) collective-permute-start(bf16[4,64,512]{2,1,0:T(8,128)(2,1)S(1)} %pad_maximum_fusion.3), channel_id=1, source_target_pairs={{0,24},{4,28},{8,16},{12,20},{16,8},{20,12},{24,0},{28,4},{1,25},{... | collective-permute-start | bytes 786440 | tf_op jit(solution)/shard_map/ppermute | solution.py:41
  58.1 18.0 %collective-permute-start.10 = (bf16[4,64,512]{2,1,0:T(8,128)(2,1)S(1)}, bf16[4,64,512]{2,1,0:T(8,128)(2,1)S(1)}, u32[]{:S(2)}, u32[]{:S(2)}) collective-permute-start(bf16[4,64,512]{2,1,0:T(8,128)(2,1)S(1)} %pad_maximum_fusion.3), channel_id=1, source_target_pairs={{0,16},{4,20},{8,24},{12,28},{16,0},{20,4},{24,8},{28,12},{1,17},{... | collective-permute-start | bytes 786440 | tf_op jit(solution)/shard_map/ppermute | solution.py:41
  59.8 16.4 %collective-permute-start.9 = (bf16[4,64,512]{2,1,0:T(8,128)(2,1)S(1)}, bf16[4,64,512]{2,1,0:T(8,128)(2,1)S(1)}, u32[]{:S(2)}, u32[]{:S(2)}) collective-permute-start(bf16[4,64,512]{2,1,0:T(8,128)(2,1)S(1)} %pad_maximum_fusion.3), channel_id=1, source_target_pairs={{0,8},{4,12},{8,0},{12,4},{16,24},{20,28},{24,16},{28,20},{1,9},{5... | collective-permute-start | bytes 786440 | tf_op jit(solution)/shard_map/ppermute | solution.py:41
  77.2 18.4 %collective-permute-start.14 = (bf16[4,128,512]{2,1,0:T(8,128)(2,1)S(1)}, bf16[4,128,512]{2,1,0:T(8,128)(2,1)S(1)}, u32[]{:S(2)}, u32[]{:S(2)}) collective-permute-start(bf16[4,128,512]{2,1,0:T(8,128)(2,1)S(1)} %pad_maximum_fusion.2), channel_id=1, source_target_pairs={{0,16},{4,20},{8,24},{12,28},{16,0},{20,4},{24,8},{28,12},{1,17},{... | collective-permute-start | bytes 1572872 | tf_op jit(solution)/shard_map/ppermute | solution.py:41
  77.9 17.7 %collective-permute-start.13 = (bf16[4,128,512]{2,1,0:T(8,128)(2,1)S(1)}, bf16[4,128,512]{2,1,0:T(8,128)(2,1)S(1)}, u32[]{:S(2)}, u32[]{:S(2)}) collective-permute-start(bf16[4,128,512]{2,1,0:T(8,128)(2,1)S(1)} %pad_maximum_fusion.2), channel_id=1, source_target_pairs={{0,8},{4,12},{8,0},{12,4},{16,24},{20,28},{24,16},{28,20},{1,9},{5... | collective-permute-start | bytes 1572872 | tf_op jit(solution)/shard_map/ppermute | solution.py:41
  80.1 25.6 %collective-permute-start.15 = (bf16[4,128,512]{2,1,0:T(8,128)(2,1)S(1)}, bf16[4,128,512]{2,1,0:T(8,128)(2,1)S(1)}, u32[]{:S(2)}, u32[]{:S(2)}) collective-permute-start(bf16[4,128,512]{2,1,0:T(8,128)(2,1)S(1)} %pad_maximum_fusion.2), channel_id=1, source_target_pairs={{0,24},{4,28},{8,16},{12,20},{16,8},{20,12},{24,0},{28,4},{1,25},{... | collective-permute-start | bytes 1572872 | tf_op jit(solution)/shard_map/ppermute | solution.py:41
  193.5 110.7 %reduce-scatter.5.cloned.1.call-start = ((), (), s32[]{:S(2)}) async-start(), calls=%async_computation.3 | async-start | bytes 983040 | tf_op jit(solution)/shard_map/reduce_scatter | solution.py:203
  212.7 31.8 %collective-permute-start.17 = (bf16[16,128,512]{2,1,0:T(8,128)(2,1)}, bf16[16,128,512]{2,1,0:T(8,128)(2,1)}, u32[]{:S(2)}, u32[]{:S(2)}) collective-permute-start(bf16[16,128,512]{2,1,0:T(8,128)(2,1)} %bitcast.198), channel_id=1, source_target_pairs={{0,4},{4,0},{8,12},{12,8},{16,20},{20,16},{24,28},{28,24},{1,5},{5... | collective-permute-start | bytes 6291464 | tf_op jit(solution)/shard_map/ppermute | solution.py:41
  242.6 35.6 %collective-permute-start.18 = (bf16[16,64,512]{2,1,0:T(8,128)(2,1)}, bf16[16,64,512]{2,1,0:T(8,128)(2,1)S(1)}, u32[]{:S(2)}, u32[]{:S(2)}) collective-permute-start(bf16[16,64,512]{2,1,0:T(8,128)(2,1)} %bitcast.204), channel_id=1, source_target_pairs={{0,4},{4,0},{8,12},{12,8},{16,20},{20,16},{24,28},{28,24},{1,5},{5... | collective-permute-start | bytes 3145736 | tf_op jit(solution)/shard_map/ppermute | solution.py:41
  246.3 31.9 %collective-permute-start.21 = (bf16[4,128,512]{2,1,0:T(8,128)(2,1)S(1)}, bf16[4,128,512]{2,1,0:T(8,128)(2,1)S(1)}, u32[]{:S(2)}, u32[]{:S(2)}) collective-permute-start(bf16[4,128,512]{2,1,0:T(8,128)(2,1)S(1)} %get-tuple-element.315), channel_id=1, source_target_pairs={{0,24},{4,28},{8,16},{12,20},{16,8},{20,12},{24,0},{28,4},{1,25},{... | collective-permute-start | bytes 1572872 | tf_op jit(solution)/shard_map/ppermute | solution.py:41
  246.4 31.8 %collective-permute-start.20 = (bf16[4,128,512]{2,1,0:T(8,128)(2,1)S(1)}, bf16[4,128,512]{2,1,0:T(8,128)(2,1)S(1)}, u32[]{:S(2)}, u32[]{:S(2)}) collective-permute-start(bf16[4,128,512]{2,1,0:T(8,128)(2,1)S(1)} %get-tuple-element.316), channel_id=1, source_target_pairs={{0,16},{4,20},{8,24},{12,28},{16,0},{20,4},{24,8},{28,12},{1,17},{... | collective-permute-start | bytes 1572872 | tf_op jit(solution)/shard_map/ppermute | solution.py:41
  249.3 29.0 %collective-permute-start.19 = (bf16[4,128,512]{2,1,0:T(8,128)(2,1)S(1)}, bf16[4,128,512]{2,1,0:T(8,128)(2,1)S(1)}, u32[]{:S(2)}, u32[]{:S(2)}) collective-permute-start(bf16[4,128,512]{2,1,0:T(8,128)(2,1)S(1)} %get-tuple-element.317), channel_id=1, source_target_pairs={{0,8},{4,12},{8,0},{12,4},{16,24},{20,28},{24,16},{28,20},{1,9},{5... | collective-permute-start | bytes 1572872 | tf_op jit(solution)/shard_map/ppermute | solution.py:41
  282.1 10.1 %collective-permute-start.31 = (bf16[4,64,512]{2,1,0:T(8,128)(2,1)S(1)}, bf16[4,64,512]{2,1,0:T(8,128)(2,1)S(1)}, u32[]{:S(2)}, u32[]{:S(2)}) collective-permute-start(bf16[4,64,512]{2,1,0:T(8,128)(2,1)S(1)} %get-tuple-element.334), channel_id=1, source_target_pairs={{0,24},{4,28},{8,16},{12,20},{16,8},{20,12},{24,0},{28,4},{1,25},{... | collective-permute-start | bytes 786440 | tf_op jit(solution)/shard_map/ppermute | solution.py:41
  283.0 14.9 %collective-permute-start.30 = (bf16[4,64,512]{2,1,0:T(8,128)(2,1)S(1)}, bf16[4,64,512]{2,1,0:T(8,128)(2,1)S(1)}, u32[]{:S(2)}, u32[]{:S(2)}) collective-permute-start(bf16[4,64,512]{2,1,0:T(8,128)(2,1)S(1)} %get-tuple-element.335), channel_id=1, source_target_pairs={{0,16},{4,20},{8,24},{12,28},{16,0},{20,4},{24,8},{28,12},{1,17},{... | collective-permute-start | bytes 786440 | tf_op jit(solution)/shard_map/ppermute | solution.py:41
  285.0 12.8 %collective-permute-start.29 = (bf16[4,64,512]{2,1,0:T(8,128)(2,1)S(1)}, bf16[4,64,512]{2,1,0:T(8,128)(2,1)S(1)}, u32[]{:S(2)}, u32[]{:S(2)}) collective-permute-start(bf16[4,64,512]{2,1,0:T(8,128)(2,1)S(1)} %get-tuple-element.336), channel_id=1, source_target_pairs={{0,8},{4,12},{8,0},{12,4},{16,24},{20,28},{24,16},{28,20},{1,9},{5... | collective-permute-start | bytes 786440 | tf_op jit(solution)/shard_map/ppermute | solution.py:41
  288.6 17.2 %collective-permute-start.25 = (bf16[4,80,512]{2,1,0:T(8,128)(2,1)S(1)}, bf16[4,80,512]{2,1,0:T(8,128)(2,1)S(1)}, u32[]{:S(2)}, u32[]{:S(2)}) collective-permute-start(bf16[4,80,512]{2,1,0:T(8,128)(2,1)S(1)} %get-tuple-element.324), channel_id=1, source_target_pairs={{0,24},{4,28},{8,16},{12,20},{16,8},{20,12},{24,0},{28,4},{1,25},{... | collective-permute-start | bytes 983048 | tf_op jit(solution)/shard_map/ppermute | solution.py:41
  289.4 21.7 %collective-permute-start.24 = (bf16[4,80,512]{2,1,0:T(8,128)(2,1)S(1)}, bf16[4,80,512]{2,1,0:T(8,128)(2,1)S(1)}, u32[]{:S(2)}, u32[]{:S(2)}) collective-permute-start(bf16[4,80,512]{2,1,0:T(8,128)(2,1)S(1)} %get-tuple-element.325), channel_id=1, source_target_pairs={{0,16},{4,20},{8,24},{12,28},{16,0},{20,4},{24,8},{28,12},{1,17},{... | collective-permute-start | bytes 983048 | tf_op jit(solution)/shard_map/ppermute | solution.py:41
  292.2 19.0 %collective-permute-start.23 = (bf16[4,80,512]{2,1,0:T(8,128)(2,1)S(1)}, bf16[4,80,512]{2,1,0:T(8,128)(2,1)S(1)}, u32[]{:S(2)}, u32[]{:S(2)}) collective-permute-start(bf16[4,80,512]{2,1,0:T(8,128)(2,1)S(1)} %get-tuple-element.326), channel_id=1, source_target_pairs={{0,8},{4,12},{8,0},{12,4},{16,24},{20,28},{24,16},{28,20},{1,9},{5... | collective-permute-start | bytes 983048 | tf_op jit(solution)/shard_map/ppermute | solution.py:41
  298.7 17.1 %collective-permute-start.32 = (bf16[192,512]{1,0:T(8,128)(2,1)}, bf16[192,512]{1,0:T(8,128)(2,1)}, u32[]{:S(2)}, u32[]{:S(2)}) collective-permute-start(bf16[192,512]{1,0:T(8,128)(2,1)} %pad_maximum_fusion.5), channel_id=1, source_target_pairs={{0,1},{1,0},{2,3},{3,2},{4,5},{5,4},{6,7},{7,6},{8,9},{9,8},{10,11... | collective-permute-start | bytes 589832 | tf_op jit(solution)/shard_map/ppermute | solution.py:44
  302.4 20.8 %collective-permute-start.33 = (bf16[192,512]{1,0:T(8,128)(2,1)}, bf16[192,512]{1,0:T(8,128)(2,1)}, u32[]{:S(2)}, u32[]{:S(2)}) collective-permute-start(bf16[192,512]{1,0:T(8,128)(2,1)} %pad_maximum_fusion.6), channel_id=1, source_target_pairs={{0,2},{1,3},{2,0},{3,1},{4,6},{5,7},{6,4},{7,5},{8,10},{9,11},{10,... | collective-permute-start | bytes 589832 | tf_op jit(solution)/shard_map/ppermute | solution.py:44
  305.8 17.3 %collective-permute-start.34 = (bf16[192,512]{1,0:T(8,128)(2,1)}, bf16[192,512]{1,0:T(8,128)(2,1)S(1)}, u32[]{:S(2)}, u32[]{:S(2)}) collective-permute-start(bf16[192,512]{1,0:T(8,128)(2,1)} %pad_maximum_fusion.7), channel_id=1, source_target_pairs={{0,3},{1,2},{2,1},{3,0},{4,7},{5,6},{6,5},{7,4},{8,11},{9,10},{10,... | collective-permute-start | bytes 589832 | tf_op jit(solution)/shard_map/ppermute | solution.py:44
  311.4 14.8 %collective-permute-start.28 = (bf16[80,512]{1,0:T(8,128)(2,1)S(1)}, bf16[80,512]{1,0:T(8,128)(2,1)S(1)}, u32[]{:S(2)}, u32[]{:S(2)}) collective-permute-start(bf16[80,512]{1,0:T(8,128)(2,1)S(1)} %get-tuple-element.321), channel_id=1, source_target_pairs={{0,3},{1,2},{2,1},{3,0},{4,7},{5,6},{6,5},{7,4},{8,11},{9,10},{10,... | collective-permute-start | bytes 245768 | tf_op jit(solution)/shard_map/ppermute | solution.py:44
  313.5 16.1 %collective-permute-start.27 = (bf16[80,512]{1,0:T(8,128)(2,1)S(1)}, bf16[80,512]{1,0:T(8,128)(2,1)S(1)}, u32[]{:S(2)}, u32[]{:S(2)}) collective-permute-start(bf16[80,512]{1,0:T(8,128)(2,1)S(1)} %get-tuple-element.322), channel_id=1, source_target_pairs={{0,2},{1,3},{2,0},{3,1},{4,6},{5,7},{6,4},{7,5},{8,10},{9,11},{10,... | collective-permute-start | bytes 245768 | tf_op jit(solution)/shard_map/ppermute | solution.py:44
  315.9 13.7 %collective-permute-start.26 = (bf16[80,512]{1,0:T(8,128)(2,1)S(1)}, bf16[80,512]{1,0:T(8,128)(2,1)S(1)}, u32[]{:S(2)}, u32[]{:S(2)}) collective-permute-start(bf16[80,512]{1,0:T(8,128)(2,1)S(1)} %get-tuple-element.323), channel_id=1, source_target_pairs={{0,1},{1,0},{2,3},{3,2},{4,5},{5,4},{6,7},{7,6},{8,9},{9,8},{10,11... | collective-permute-start | bytes 245768 | tf_op jit(solution)/shard_map/ppermute | solution.py:44
  (39 other events, 457.1 us)
Sparse Core Ops, SparseCore 0:
  12.0 84.6 all-gather.2
  193.6 77.1 reduce-scatter.2
  280.3 23.4 reduce-scatter.4
